TPU v7x, 256 devices: a whole 4x4x8 slice. The times are simulated.
256 devices in a mesh: dp: 16 (over z_hi, y), expert: 16 (over z_lo, x, core).
Axes of the slice: x: 4, y: 4, z: 8 (z_hi: 4, z_lo: 2; z = z_hi * 2 + z_lo), core: 2. Of those that a mesh axis runs over, the one named last changes fastest.
Arguments:
- patches: bfloat16 [512, 256, 1280], P(('dp', 'expert')), may hold values from -12 to 12
- cotangent: bfloat16 [512, 256, 1280], P(('dp', 'expert')), may hold values from -6 to 6
- other_logsum: float32 [512, 256], P(('dp', 'expert')), may hold values from 6 to 9
- slot_keys: bfloat16 [32, 1280], replicated, may hold values from -0.25 to 0.25
- w_in: bfloat16 [32, 1280, 5120], P('expert', None, 'dp'), may hold values from -0.15625 to 0.15625
- w_out: bfloat16 [32, 5120, 1280], P('expert', 'dp'), may hold values from -0.078125 to 0.078125
Outputs:
- patch_grad: bfloat16 [512, 256, 1280], P(('dp', 'expert'))
- key_grad: float32 [32, 1280], replicated
- w_in_grad: bfloat16 [32, 1280, 5120], P('expert', None, 'dp')
- w_out_grad: bfloat16 [32, 5120, 1280], P('expert', 'dp')
All inputs are finite; a program needn't handle non-finite values.
Results may differ from a plain program's by a relative error of at most 0.03.
Values may be sent and summed in bfloat16 or wider, within the bound.
A program may use at most 128 MiB of HBM per device.

v0:
```python
import jax
import jax.numpy as jnp
from jax import lax
from jax.sharding import PartitionSpec as P


def expert_side(slot_rows, grad_rows, w_in, w_out):
    hidden = jnp.einsum("bed,edf->bef", slot_rows, w_in, preferred_element_type=jnp.float32)
    upstream = jnp.einsum("bed,efd->bef", grad_rows, w_out, preferred_element_type=jnp.float32)
    activated, pullback = jax.vjp(jax.nn.gelu, hidden)
    act_half = activated.astype(jnp.bfloat16)
    pre_half = pullback(upstream)[0].astype(jnp.bfloat16)
    w_out_grad = jnp.einsum(
        "bef,bed->efd", act_half, grad_rows, preferred_element_type=jnp.float32
    ).astype(jnp.bfloat16)
    w_in_grad = jnp.einsum(
        "bed,bef->edf", slot_rows, pre_half, preferred_element_type=jnp.float32
    ).astype(jnp.bfloat16)
    return (act_half, pre_half, w_in_grad, w_out_grad)


def expert_terms(act_half, pre_half, w_in, w_out):
    outputs = jnp.einsum("bef,efd->bed", act_half, w_out, preferred_element_type=jnp.float32)
    inputs_grad = jnp.einsum("bef,edf->bed", pre_half, w_in, preferred_element_type=jnp.float32)
    return jnp.stack((outputs, inputs_grad), axis=1)


def on_device(patches, cotangent, other_logsum, slot_keys, w_in, w_out):
    logits = jnp.einsum("imd,sd->ism", patches, slot_keys, preferred_element_type=jnp.float32)
    exponent = jnp.exp(logits)
    dispatch = exponent / jnp.sum(exponent, axis=2, keepdims=True)
    combine = exponent / (
        jnp.sum(exponent, axis=1, keepdims=True) + jnp.exp(other_logsum)[:, None, :]
    )
    dispatch_half = dispatch.astype(jnp.bfloat16)
    combine_half = combine.astype(jnp.bfloat16)
    slot_in = jnp.einsum(
        "ism,imd->isd", dispatch_half, patches, preferred_element_type=jnp.float32
    ).astype(jnp.bfloat16)
    slot_grad = jnp.einsum(
        "ism,imd->isd", combine_half, cotangent, preferred_element_type=jnp.float32
    ).astype(jnp.bfloat16)
    collected = (
        lax.all_gather(slot_in, "dp", axis=0, tiled=True),
        lax.all_gather(slot_grad, "dp", axis=0, tiled=True),
    )
    spread = (
        lax.all_to_all(collected[0], "expert", split_axis=1, concat_axis=0, tiled=True),
        lax.all_to_all(collected[1], "expert", split_axis=1, concat_axis=0, tiled=True),
    )
    act_half, pre_half, w_in_grad, w_out_grad = expert_side(spread[0], spread[1], w_in, w_out)
    partial_half = expert_terms(act_half, pre_half, w_in, w_out).astype(jnp.bfloat16)
    returned = lax.all_to_all(partial_half, "expert", split_axis=0, concat_axis=2, tiled=True)
    summed = lax.psum_scatter(
        returned.astype(jnp.float32).astype(jnp.bfloat16), "dp", scatter_dimension=0, tiled=True
    )
    slot_out = summed[:, 0]
    slot_in_grad = summed[:, 1]
    comb_grad = jnp.einsum("imd,isd->ism", cotangent, slot_out, preferred_element_type=jnp.float32)
    disp_grad = jnp.einsum(
        "imd,isd->ism", patches, slot_in_grad, preferred_element_type=jnp.float32
    )
    logit_grad = combine * (comb_grad - jnp.sum(combine * comb_grad, axis=1, keepdims=True))
    logit_grad = logit_grad + dispatch * (
        disp_grad - jnp.sum(dispatch * disp_grad, axis=2, keepdims=True)
    )
    logit_half = logit_grad.astype(jnp.bfloat16)
    patch_grad = jnp.einsum(
        "ism,isd->imd", dispatch_half, slot_in_grad, preferred_element_type=jnp.float32
    )
    patch_grad = patch_grad + jnp.einsum(
        "ism,sd->imd", logit_half, slot_keys, preferred_element_type=jnp.float32
    )
    key_local = jnp.einsum("ism,imd->sd", logit_half, patches, preferred_element_type=jnp.float32)
    key_grad = lax.psum(key_local, ("dp", "expert"))
    return (patch_grad.astype(jnp.bfloat16), key_grad, w_in_grad, w_out_grad)


def solution(mesh):
    placed = (
        P(("dp", "expert"), None, None),
        P(("dp", "expert"), None, None),
        P(("dp", "expert"), None),
        P(),
        P("expert", None, "dp"),
        P("expert", "dp", None),
    )
    return jax.shard_map(
        on_device,
        mesh=mesh,
        in_specs=placed,
        out_specs=(
            P(("dp", "expert"), None, None),
            P(),
            P("expert", None, "dp"),
            P("expert", "dp", None),
        ),
        check_vma=False,
    )
```

profile of v0, /device:TPU:1, one launch (start us, length us, event | category | flops | bytes accessed | tf_op | source)
XLA Modules:
  0.0 819.4 jit_solution(6913701063364891074)
XLA Ops:
  7.2 0.0 copy-start
  7.2 0.0 copy-start.2
  7.2 0.0 copy-start.10
  7.2 0.0 all-gather.5.cloned.1.call-start
  7.2 2.0 fusion.41
  9.3 0.0 copy-done.10
  9.3 2.3 convolution_convert_fusion.4
  11.6 0.0 all-gather.5.cloned.1.call-update
  11.6 0.0 all-gather.3.cloned.1.call-start
  11.7 0.0 copy-done.2
  11.7 1.1 convolution_convert_fusion.5
  12.8 0.0 all-gather.3.cloned.1.call-update
  12.8 65.8 %all-gather.5.cloned.1.call-done = bf16[32,32,1280]{2,1,0:T(8,128)(2,1)} async-done(((bf16[2,32,1280]{2,1,0:T(8,128)(2,1)}), bf16[32,32,1280]{2,1,0:T(8,128)(2,1)}) %all-gather.5.cloned.1.call-update) | async-done | bytes 2621456 | tf_op jit(solution)/shard_map/all_gather | solution.py:45
  78.6 4.7 copy.15
  83.4 5.2 all-to-all-start.1
  88.5 60.2 %all-gather.3.cloned.1.call-done = bf16[32,32,1280]{2,1,0:T(8,128)(2,1)} async-done(((bf16[2,32,1280]{2,1,0:T(8,128)(2,1)}), bf16[32,32,1280]{2,1,0:T(8,128)(2,1)}) %all-gather.3.cloned.1.call-update) | async-done | bytes 2621456 | tf_op jit(solution)/shard_map/all_gather | solution.py:44
  148.8 4.7 copy.13
  153.5 0.0 all-to-all-done.1
  153.5 5.7 all-to-all-start
  159.1 0.2 all-reduce.6.cloned.1.call-start
  159.3 3.5 copy.16
  162.8 30.0 %all-to-all-done = bf16[32,32,1280]{2,0,1:T(8,128)(2,1)} async-done(((bf16[32,32,1280]{2,0,1:T(8,128)(2,1)}), bf16[32,32,1280]{2,0,1:T(8,128)(2,1)}, u32[]{:S(2)}, u32[]{:S(2)}) %all-to-all-start) | async-done | bytes 2621472 | tf_op jit(solution)/shard_map/all_to_all | solution.py:48
  192.8 2.0 copy.14
  194.9 0.0 copy-start.3
  194.9 0.2 copy-done.11
  195.1 1.0 convolution_bitcast_fusion.2
  196.1 0.3 copy-done.3
  196.4 0.0 copy-done
  196.4 1.6 fusion.2
  198.0 0.0 copy-done.13
  198.0 0.6 copy-done.5
  198.6 1.6 fusion.11
  200.2 0.0 copy-start.7
  200.2 0.8 copy-done.7
  201.0 1.6 fusion.3
  202.6 2.8 pad_maximum_fusion
  205.4 10.2 %copy.17 = bf16[512,2,2,1280]{3,2,1,0:T(2,128)(2,1)} copy(bf16[512,2,2,1280]{3,0,2,1:T(8,128)(2,1)} %pad_maximum_fusion) | data formatting | bytes 10485760 | tf_op jit(solution)/shard_map/stack | solution.py:25
  215.6 69.2 %all_to_all.54 = bf16[512,2,2,1280]{3,2,1,0:T(2,128)(2,1)} all-to-all(bf16[512,2,2,1280]{3,2,1,0:T(2,128)(2,1)} %copy.17), channel_id=1, replica_groups=mesh['dp'=16,'expert'=16] {'expert'}, dimensions={0} | all-to-all | bytes 10485760 | tf_op jit(solution)/shard_map/all_to_all | solution.py:53
  284.7 10.5 %copy.18 = bf16[32,2,16,2,1280]{4,3,2,0,1:T(2,128)(2,1)} copy(bf16[32,2,16,2,1280]{4,3,1,0,2:T(2,128)(2,1)} %bitcast.71) | data formatting | bytes 10485760 | tf_op jit(solution)/shard_map/all_to_all | solution.py:53
  295.3 11.6 %all_to_all.50 = bf16[32,2,32,1280]{3,2,0,1:T(8,128)(2,1)} reshape(bf16[32,2,16,2,1280]{4,3,2,0,1:T(2,128)(2,1)} %copy.18) | data formatting | bytes 10485760 | tf_op jit(solution)/shard_map/all_to_all | solution.py:53
  306.9 0.0 all-reduce.6.cloned.1.call-update
  306.9 0.0 all-reduce.4.cloned.1.call-start
  307.0 0.6 copy-done.12
  307.6 0.6 dynamic-slice
  308.8 0.2 fusion.31
  309.0 0.0 copy-done.8
  309.0 0.0 copy-start.14
  309.0 4.1 convolution_convert_fusion.2
  313.1 0.0 copy-done.6
  313.1 2.3 convolution_convert_fusion.3
  315.4 248.2 %all-reduce.6.cloned.1.call-done = bf16[32,2,32,1280]{3,2,0,1:T(8,128)(2,1)} async-done(((bf16[32,2,32,1280]{3,2,0,1:T(8,128)(2,1)}), bf16[32,2,32,1280]{3,2,0,1:T(8,128)(2,1)}) %all-reduce.6.cloned.1.call-update) | async-done | bytes 5242896
  563.6 1.4 fusion.21
  565.0 0.2 fusion.17
  565.2 0.0 copy-done.4
  565.2 0.0 copy-start.9
  565.2 1.4 fusion.20
  566.6 1.0 convolution_bitcast_fusion
  567.6 0.0 copy-done.9
  567.6 2.0 fusion.19
  569.7 0.0 all-reduce.4.cloned.1.call-update
  569.7 0.0 copy-start.1
  569.7 3.6 fusion.4
  573.3 237.9 %all-reduce.4.cloned.1.call-done = f32[32,1280]{1,0:T(8,128)} async-done(((f32[32,1280]{1,0:T(8,128)}), f32[32,1280]{1,0:T(8,128)}) %all-reduce.4.cloned.1.call-update) | async-done | bytes 163856 | tf_op jit(solution)/shard_map/psum | solution.py:75
  811.2 1.6 copy.23
  (10 shorter events, 0.0 us)
Async XLA Ops:
  7.2 189.2 %copy-start = (bf16[2,320,1280]{2,1,0:T(8,128)(2,1)S(1)}, bf16[2,320,1280]{2,1,0:T(8,128)(2,1)}, u32[]{:S(2)}) copy-start(bf16[2,320,1280]{2,1,0:T(8,128)(2,1)} %param.11) | copy-start | bytes 4915204
  7.2 4.5 copy-start.2
  7.2 2.1 copy-start.10
  7.2 71.4 %all-gather.5.cloned.1.call-start = ((), (), s32[]{:S(2)}) async-start(), calls=%async_computation.4 | async-start | bytes 2785280 | tf_op jit(solution)/shard_map/all_gather | solution.py:45
  11.6 137.1 %all-gather.3.cloned.1.call-start = ((), (), s32[]{:S(2)}) async-start(), calls=%async_computation.3 | async-start | bytes 2785280 | tf_op jit(solution)/shard_map/all_gather | solution.py:44
  83.4 70.1 %all-to-all-start.1 = ((bf16[32,32,1280]{2,0,1:T(8,128)(2,1)}), bf16[32,32,1280]{2,0,1:T(8,128)(2,1)}, u32[]{:S(2)}, u32[]{:S(2)}) async-start(bf16[32,32,1280]{2,0,1:T(8,128)(2,1)} %copy.15), calls=%async_computation.1 | async-start | bytes 5242880 | tf_op jit(solution)/shard_map/all_to_all | solution.py:49
  153.5 39.4 %all-to-all-start = ((bf16[32,32,1280]{2,0,1:T(8,128)(2,1)}), bf16[32,32,1280]{2,0,1:T(8,128)(2,1)}, u32[]{:S(2)}, u32[]{:S(2)}) async-start(bf16[32,32,1280]{2,0,1:T(8,128)(2,1)} %copy.13), calls=%async_computation | async-start | bytes 5242880 | tf_op jit(solution)/shard_map/all_to_all | solution.py:48
  159.1 404.5 %all-reduce.6.cloned.1.call-start = ((), (), s32[]{:S(2)}) async-start(), calls=%async_computation.6 | async-start | bytes 10485760
  192.8 2.2 copy-start.11
  194.9 1.5 copy-start.3
  196.4 1.6 copy-start.13
  196.4 2.2 copy-start.5
  200.2 0.8 copy-start.7
  306.9 0.7 copy-start.12
  306.9 2.1 copy-start.8
  306.9 504.3 %all-reduce.4.cloned.1.call-start = ((), (), s32[]{:S(2)}) async-start(), calls=%async_computation.5 | async-start | bytes 327680 | tf_op jit(solution)/shard_map/psum | solution.py:75
  309.0 4.1 copy-start.6
  309.0 4.1 copy-start.14
  315.4 249.8 %copy-start.4 = (bf16[2,256,1280]{2,1,0:T(8,128)(2,1)S(1)}, bf16[2,256,1280]{2,1,0:T(8,128)(2,1)}, u32[]{:S(2)}) copy-start(bf16[2,256,1280]{2,1,0:T(8,128)(2,1)} %param.7) | copy-start | bytes 3932164
  565.2 2.5 copy-start.9
  569.7 243.1 %copy-start.1 = (bf16[2,320,1280]{2,1,0:T(8,128)(2,1)S(1)}, bf16[2,320,1280]{2,1,0:T(8,128)(2,1)}, u32[]{:S(2)}) copy-start(bf16[2,320,1280]{2,1,0:T(8,128)(2,1)} %param.11) | copy-start | bytes 4915204
Sparse Core Ops, SparseCore 0:
  11.8 66.8 all-gather.4
  81.6 67.1 all-gather.2
  307.1 256.4 all-reduce.5
  569.8 241.3 all-reduce.3
where the time goes:
time: 820 us; the launch traced here: 819 us
  waiting for transfers between devices  642 us (78%)
  blocking collectives  69.2 us (8%)
  local copies, waits for them, and re-layouts  51.9 us (6%)
  matrix products  27.1 us (3%)
  between operations  14.6 us (2%)
  starting transfers between devices  11.2 us (1%)
    unnamed x5, waiting for transfers between devices  248 us
    psum x1, waiting for transfers between devices, on_device(): key_grad = lax.psum(key_local, ('dp', 'expert'))  238 us
    all_to_all x1, blocking collectives, on_device(): lax.all_to_all(partial_half, 'expert', split_axis=0, concat_axis=2, tiled...  69.2 us
    all_gather x1, waiting for transfers between devices, on_device(): lax.all_gather(slot_grad, 'dp', axis=0, tiled=True)  65.8 us
    all_gather x1, waiting for transfers between devices, on_device(): lax.all_gather(slot_in, 'dp', axis=0, tiled=True)  60.2 us
    all_to_all x1, waiting for transfers between devices, on_device(): lax.all_to_all(collected[0], 'expert', split_axis=1, concat_axis=0, tiled...  30 us
    all_to_all x2, local copies, waits for them, and re-layouts, on_device(): lax.all_to_all(partial_half, 'expert', split_axis=0, concat_axis=2, tiled...  22.2 us
  transfers between devices with their start and end apart: 6, of which 5 were waited for; matrix products, arithmetic and copies ran while one was open for 3% of the time, Pallas kernels for 0%

commit v1 on v0

v1 whole, which is shorter than its diff:
```python
import functools

import jax
import jax.numpy as jnp
from jax import lax
from jax.experimental import pallas as pl
from jax.experimental.pallas import tpu as pltpu
from jax.sharding import PartitionSpec as P

MESH = pl.DeviceIdType.MESH
BF = jnp.bfloat16
F32 = jnp.float32

D = 1280
FB = 320
SPLIT = 1024
COLS = ((0, SPLIT), (SPLIT, D - SPLIT))
N_SEM = 224
GELU_C = 0.7978845608028654
GELU_A = 0.044715


def dot(a, b):
    return lax.dot_general(a, b, (((1,), (0,)), ((), ())), preferred_element_type=F32)


def dot_nt(a, b):
    return lax.dot_general(a, b, (((1,), (1,)), ((), ())), preferred_element_type=F32)


def dot_tn(a, b):
    return lax.dot_general(a, b, (((0,), (0,)), ((), ())), preferred_element_type=F32)


def iota(shape, dim):
    return lax.broadcasted_iota(jnp.int32, shape, dim)


def piece_row(slot_off, half, k, t, i):
    return slot_off * 16 + half * 8 + k * 4 + t * 2 + i


def spread_index(r, me):
    off, k, t, i = r >> 4, (r >> 2) & 1, (r >> 1) & 1, r & 1
    owner = (me + off) & 15
    return (t * 2 + i) * 32 + 2 * owner + k


def block_index(r):
    off, k, t, i = r >> 4, (r >> 2) & 1, (r >> 1) & 1, r & 1
    return (k * 2 + t) * 32 + off * 2 + i


def one_hot(index_of, half, rows_are_pieces):
    shape = (256, 128) if rows_are_pieces else (128, 256)
    piece = iota(shape, 0 if rows_are_pieces else 1)
    other = iota(shape, 1 if rows_are_pieces else 0)
    hit = (index_of(piece) == other) & (((piece >> 3) & 1) == half)
    return jnp.where(hit, 1.0, 0.0).astype(BF)


def kernel(
    patches_hbm, cot_hbm, ols_ref, keys_ref, win_hbm, wout_hbm,
    pg_hbm, kg_ref, wig_hbm, wog_hbm,
    patches, cot, win, wout, pg, wig, wog,
    disp_s, comb_s, g, pt, act_s, pre_s, r1, r2,
    a2s, a2r, b2s, b2r, ks, k1, k2, k3, k4,
    send_sem, recv_sem, in_sem, out_sem,
):
    dp = lax.axis_index("dp")
    me = lax.axis_index("expert")
    zh, y = dp // 4, dp % 4

    def expert_peer(off):
        return (dp, lax.rem(me + off, 16))

    def dp_peer(off):
        return (lax.rem(dp + off, 16), me)

    def ring_peer(axis, step):
        if axis == "y":
            return (zh * 4 + lax.rem(y + step + 4, 4), me)
        return (lax.rem(zh + step + 4, 4) * 4 + y, me)

    barrier = pltpu.get_barrier_semaphore()
    for off in range(1, 16):
        pl.semaphore_signal(barrier, inc=1, device_id=expert_peer(off), device_id_type=MESH)
        pl.semaphore_signal(barrier, inc=1, device_id=dp_peer(off), device_id_type=MESH)

    loads = {}
    for n, (name, src, dst) in enumerate(
        (("x", patches_hbm, patches), ("c", cot_hbm, cot), ("wi", win_hbm, win), ("wo", wout_hbm, wout))
    ):
        loads[name] = pltpu.make_async_copy(src, dst, in_sem.at[n])
        loads[name].start()

    copies = {}

    def send(name, src, dst, device):
        n = len(copies)
        assert n < N_SEM
        copy = pltpu.make_async_remote_copy(
            src_ref=src, dst_ref=dst, send_sem=send_sem.at[n], recv_sem=recv_sem.at[n],
            device_id=device, device_id_type=MESH,
        )
        copy.start()
        copies[name] = copy

    def got(*name):
        copies[name].wait_recv()

    keys = keys_ref[...]
    loads["x"].wait()
    loads["c"].wait()
    rows_in, rows_grad = [], []
    for i in range(2):
        exponent = jnp.exp(dot_nt(keys, patches[i]))
        dispatch = exponent / jnp.sum(exponent, axis=1, keepdims=True)
        combine = exponent / (jnp.sum(exponent, axis=0, keepdims=True) + jnp.exp(ols_ref[i]))
        disp_s[i] = dispatch
        comb_s[i] = combine
        rows_in.append(dot(dispatch.astype(BF), patches[i]).astype(BF))
        rows_grad.append(dot(combine.astype(BF), cot[i]).astype(BF))
    rows = jnp.concatenate(rows_in + rows_grad, axis=0)

    def to_pieces(rows, index_of, dst):
        half = D // 2
        pieces = dot(one_hot(index_of, 0, True), rows[:, :half]) + dot(
            one_hot(index_of, 1, True), rows[:, half:]
        )
        dst[...] = pieces.astype(BF).reshape(16, 16, half)

    def from_pieces(src, index_of, half):
        pieces = src[...].reshape(256, D // 2)
        return dot(one_hot(index_of, half, False), pieces).astype(BF)

    spread = functools.partial(spread_index, me=me)
    to_pieces(rows, spread, a2s)
    a2r[0] = a2s[0]
    pl.semaphore_wait(barrier, 30)
    for off in range(1, 16):
        send(("a", off), a2s.at[off], a2r.at[off], expert_peer(off))
    for off in range(1, 16):
        got("a", off)
    for half in range(2):
        cols = slice(half * 640, half * 640 + 640)
        g[:, 0, 0, :, cols] = from_pieces(a2r, block_index, half).reshape(4, 32, 640)

    def at(ref, part, k, a1, a2, r0=0, nr=32):
        c0, nc = COLS[part]
        dy, dz = (a2, a1) if part == 0 else (a1, a2)
        return ref.at[pl.ds(2 * k, 2), dy, dz, pl.ds(r0, nr), pl.ds(c0, nc)]

    AXES = (("z", "y"), ("y", "z"))

    def ag1(part, k):
        axis = AXES[part][0]
        for step, a in ((1, 3), (-1, 1)):
            send(("p1", part, k, step), at(g, part, k, 0, 0), at(g, part, k, a, 0), ring_peer(axis, step))

    def ag1_relay(part, k):
        axis = AXES[part][0]
        for step, a, r in ((1, 3, 0), (-1, 1, 16)):
            got("p1", part, k, step)
            send(("r1", part, k, step), at(g, part, k, a, 0, r, 16), at(g, part, k, 2, 0, r, 16), ring_peer(axis, step))

    def ag1_done(part, k):
        got("r1", part, k, 1)
        got("r1", part, k, -1)

    def ag2(part, k, a1):
        axis = AXES[part][1]
        for step, a in ((1, 3), (-1, 1)):
            send(("p2", part, k, a1, step), at(g, part, k, a1, 0), at(g, part, k, a1, a), ring_peer(axis, step))

    def ag2_relay(part, k, a1):
        axis = AXES[part][1]
        for step, a, r in ((1, 3, 0), (-1, 1, 16)):
            got("p2", part, k, a1, step)
            send(("r2", part, k, a1, step), at(g, part, k, a1, a, r, 16), at(g, part, k, a1, 2, r, 16), ring_peer(axis, step))

    def ag2_done(part, k, a1):
        got("r2", part, k, a1, 1)
        got("r2", part, k, a1, -1)

    def expert(k, dy):
        x0 = g[2 * k, dy].reshape(128, D)
        x1 = g[2 * k + 1, dy].reshape(128, D)
        hidden = dot(x0, win[k])
        upstream = dot_nt(x1, wout[k])
        square = hidden * hidden
        tanh = jnp.tanh(GELU_C * (hidden + GELU_A * square * hidden))
        act = (0.5 * hidden * (1.0 + tanh)).astype(BF)
        slope = 0.5 * (1.0 + tanh) + (0.5 * hidden) * (1.0 - tanh * tanh) * (
            GELU_C + (3.0 * GELU_C * GELU_A) * square
        )
        pre = (slope * upstream).astype(BF)
        act_s[k, dy * 128 : dy * 128 + 128, :] = act
        pre_s[k, dy * 128 : dy * 128 + 128, :] = pre
        pt[2 * k, dy] = dot(act, wout[k]).astype(BF).reshape(4, 32, D)
        pt[2 * k + 1, dy] = dot_nt(pre, win[k]).astype(BF).reshape(4, 32, D)

    def weight_grads(k):
        wog[k] = dot_tn(act_s[k], g[2 * k + 1].reshape(512, D)).astype(BF)
        wig[k] = dot_tn(g[2 * k].reshape(512, D), pre_s[k]).astype(BF)
        for n, (src, dst) in enumerate(((wig, wig_hbm), (wog, wog_hbm))):
            stores.append(pltpu.make_async_copy(src.at[k], dst.at[k], out_sem.at[2 * k + n]))
            stores[-1].start()

    stores = []

    UP, TP, MP, UM, TM, MM = range(6)

    def wide(ref, part, k, a2, r0):
        c0, nc = COLS[part]
        if part == 0:
            return ref.at[pl.ds(2 * k, 2), a2, :, pl.ds(r0, 16), pl.ds(c0, nc)]
        return ref.at[pl.ds(2 * k, 2), :, a2, pl.ds(r0, 16), pl.ds(c0, nc)]

    def land(ph, part, k, m):
        c0, nc = COLS[part]
        if ph == 1:
            return r1.at[k, m, :, :, :, pl.ds(c0, nc)]
        return r2.at[k, m, :, :, pl.ds(c0, nc)]

    def part_of(ph, part, k, a, r0):
        if ph == 1:
            return wide(pt, part, k, a, r0)
        return at(pt, part, k, a, 0, r0, 16)

    def rs_send(ph, part, k, m, a, r0):
        axis = AXES[part][2 - ph]
        step = 1 if m < 3 else -1
        send(("rs", ph, part, k, m), part_of(ph, part, k, a, r0), land(ph, part, k, m), ring_peer(axis, step))

    def rs_u(ph, part, k):
        rs_send(ph, part, k, UP, 1, 0)
        rs_send(ph, part, k, UM, 3, 16)

    def rs_t(ph, part, k):
        rs_send(ph, part, k, TP, 2, 16)
        rs_send(ph, part, k, TM, 2, 0)

    def add_into(dst, *srcs):
        total = dst[...].astype(F32)
        for src in srcs:
            total = total + src[...].astype(F32)
        dst[...] = total.astype(BF)

    def rs_m(ph, part, k):
        for t, m, a, r0 in ((TP, MP, 1, 16), (TM, MM, 3, 0)):
            got("rs", ph, part, k, t)
            add_into(part_of(ph, part, k, a, r0), land(ph, part, k, t))
            rs_send(ph, part, k, m, a, r0)

    def rs_final(ph, part, k):
        for u, m, r0 in ((UP, MM, 0), (UM, MP, 16)):
            got("rs", ph, part, k, u)
            got("rs", ph, part, k, m)
            add_into(part_of(ph, part, k, 0, r0), land(ph, part, k, u), land(ph, part, k, m))

    A, B = 0, 1
    ag1(A, 0)
    ag1(B, 0)
    ag2(A, 0, 0)
    ag2(B, 0, 0)
    ag1_relay(B, 0)
    ag2(B, 0, 3)
    ag2(B, 0, 1)
    ag2(A, 1, 0)
    ag2_relay(A, 0, 0)
    ag1_relay(A, 0)
    ag2(A, 0, 3)
    ag2(A, 0, 1)
    ag1(A, 1)
    ag1(B, 1)
    ag2_relay(A, 1, 0)
    ag1_done(B, 0)
    ag2(B, 0, 2)
    ag2_relay(B, 0, 0)
    ag2_relay(B, 0, 3)
    ag2_relay(B, 0, 1)
    ag1_done(A, 0)
    ag2(A, 0, 2)
    ag2_relay(A, 0, 3)
    ag2_relay(A, 0, 1)
    ag2_relay(B, 0, 2)
    ag1_relay(B, 1)
    ag2(B, 1, 0)
    ag2(B, 1, 3)
    ag2(B, 1, 1)
    ag2_done(B, 0, 0)
    loads["wi"].wait()
    loads["wo"].wait()
    expert(0, 0)
    ag2_relay(A, 0, 2)
    ag1_relay(A, 1)
    ag2(A, 1, 3)
    ag2(A, 1, 1)
    ag1_done(B, 1)
    ag2(B, 1, 2)
    ag2_done(B, 0, 3)
    expert(0, 3)
    ag2_relay(B, 1, 0)
    ag2_relay(B, 1, 3)
    ag2_relay(B, 1, 1)
    ag1_done(A, 1)
    ag2(A, 1, 2)
    ag2_done(B, 0, 1)
    expert(0, 1)
    ag2_relay(A, 1, 3)
    ag2_relay(A, 1, 1)
    ag2_relay(B, 1, 2)
    for a in (0, 3, 1, 2):
        ag2_done(A, 0, a)
    ag2_done(B, 0, 2)
    rs_u(1, A, 0)
    expert(0, 2)
    rs_t(1, A, 0)
    rs_t(1, B, 0)
    rs_u(1, B, 0)
    ag2_relay(A, 1, 2)
    ag2_done(B, 1, 0)
    expert(1, 0)
    rs_m(1, A, 0)
    rs_m(1, B, 0)
    ag2_done(B, 1, 3)
    expert(1, 3)
    ag2_done(B, 1, 1)
    expert(1, 1)
    rs_u(1, A, 1)
    for a in (0, 3, 1, 2):
        ag2_done(A, 1, a)
    ag2_done(B, 1, 2)
    expert(1, 2)
    rs_t(1, A, 1)
    rs_t(1, B, 1)
    rs_u(1, B, 1)
    for part in (B, A):
        rs_final(1, part, 0)
        rs_t(2, part, 0)
        rs_u(2, part, 0)
    rs_m(1, A, 1)
    rs_m(1, B, 1)
    weight_grads(0)
    rs_m(2, B, 0)
    rs_m(2, A, 0)
    weight_grads(1)
    for part in (B, A):
        rs_final(1, part, 1)
        rs_t(2, part, 1)
        rs_u(2, part, 1)
    rs_final(2, B, 0)
    rs_final(2, A, 0)
    rs_m(2, B, 1)
    rs_m(2, A, 1)
    rs_final(2, B, 1)
    rs_final(2, A, 1)

    to_pieces(pt[:, 0, 0].reshape(128, D), block_index, b2s)
    b2r[0] = b2s[0]
    for off in range(1, 16):
        send(("b", off), b2s.at[off], b2r.at[off], expert_peer(16 - off))
    for off in range(1, 16):
        got("b", off)
    back = jnp.concatenate([from_pieces(b2r, spread, half) for half in range(2)], axis=1)

    halves = []
    key_part = jnp.zeros((32, D), F32)
    for i in range(2):
        slot_out = back[i * 32 : i * 32 + 32]
        slot_in_grad = back[64 + i * 32 : 96 + i * 32]
        comb_grad = dot_nt(slot_out, cot[i])
        disp_grad = dot_nt(slot_in_grad, patches[i])
        dispatch = disp_s[i]
        combine = comb_s[i]
        logit_grad = combine * (comb_grad - jnp.sum(combine * comb_grad, axis=0, keepdims=True))
        logit_grad = logit_grad + dispatch * (
            disp_grad - jnp.sum(dispatch * disp_grad, axis=1, keepdims=True)
        )
        logit_half = logit_grad.astype(BF)
        key_part = key_part + dot(logit_half, patches[i])
        halves.append((dispatch.astype(BF), logit_half, slot_in_grad))

    for o in range(16):
        rg, c0 = o // 4, (o % 4) * 384
        nc = min(384, D - c0)
        ks[o, :, :nc] = key_part[rg * 8 : rg * 8 + 8, c0 : c0 + nc]
        if nc < 384:
            ks[o, :, nc:] = jnp.zeros((8, 384 - nc), F32)
    for off in range(1, 16):
        send(("k1", off), ks.at[lax.rem(me + off, 16)], k1.at[off], expert_peer(off))

    def image_out(i):
        dispatch_half, logit_half, slot_in_grad = halves[i]
        lhs = jnp.concatenate([dispatch_half, logit_half], axis=0)
        rhs = jnp.concatenate([slot_in_grad, keys], axis=0)
        pg[i] = dot_tn(lhs, rhs).astype(BF)
        stores.append(pltpu.make_async_copy(pg.at[i], pg_hbm.at[i], out_sem.at[4 + i]))
        stores[-1].start()

    image_out(0)
    total = ks[me]
    for off in range(1, 16):
        got("k1", off)
        total = total + k1[off]
    k2[0] = total
    for off in range(1, 16):
        send(("k2", off), k2.at[0], k2.at[off], dp_peer(off))
    image_out(1)
    for off in range(1, 16):
        got("k2", off)
    total = k2[lax.rem(dp, 16)]
    for n in range(1, 16):
        total = total + k2[lax.rem(dp + 16 - n, 16)]
    k3[0] = total
    for off in range(1, 16):
        send(("k3", off), k3.at[0], k3.at[off], expert_peer(off))
    k4[me] = total
    for off in range(1, 16):
        got("k3", off)
        k4[lax.rem(me + 16 - off, 16)] = k3[off]
    for o in range(16):
        rg, c0 = o // 4, (o % 4) * 384
        nc = min(384, D - c0)
        kg_ref[rg * 8 : rg * 8 + 8, c0 : c0 + nc] = k4[o, :, :nc]
    for store in stores:
        store.wait()
    for copy in copies.values():
        copy.wait_send()


def on_device(patches, cotangent, other_logsum, slot_keys, w_in, w_out):
    any_spec = pl.BlockSpec(memory_space=pl.ANY)
    vmem = pl.BlockSpec(memory_space=pltpu.VMEM)
    return pl.pallas_call(
        kernel,
        out_shape=(
            jax.ShapeDtypeStruct((2, 256, D), BF),
            jax.ShapeDtypeStruct((32, D), F32),
            jax.ShapeDtypeStruct((2, D, FB), BF),
            jax.ShapeDtypeStruct((2, FB, D), BF),
        ),
        in_specs=[any_spec, any_spec, vmem, vmem, any_spec, any_spec],
        out_specs=(any_spec, vmem, any_spec, any_spec),
        scratch_shapes=[
            pltpu.VMEM((2, 256, D), BF),
            pltpu.VMEM((2, 256, D), BF),
            pltpu.VMEM((2, D, FB), BF),
            pltpu.VMEM((2, FB, D), BF),
            pltpu.VMEM((2, 256, D), BF),
            pltpu.VMEM((2, D, FB), BF),
            pltpu.VMEM((2, FB, D), BF),
            pltpu.VMEM((2, 32, 256), F32),
            pltpu.VMEM((2, 32, 256), F32),
            pltpu.VMEM((4, 4, 4, 32, D), BF),
            pltpu.VMEM((4, 4, 4, 32, D), BF),
            pltpu.VMEM((2, 512, FB), BF),
            pltpu.VMEM((2, 512, FB), BF),
            pltpu.VMEM((2, 6, 2, 4, 16, D), BF),
            pltpu.VMEM((2, 6, 2, 16, D), BF),
            pltpu.VMEM((16, 16, D // 2), BF),
            pltpu.VMEM((16, 16, D // 2), BF),
            pltpu.VMEM((16, 16, D // 2), BF),
            pltpu.VMEM((16, 16, D // 2), BF),
            pltpu.VMEM((16, 8, 384), F32),
            pltpu.VMEM((16, 8, 384), F32),
            pltpu.VMEM((16, 8, 384), F32),
            pltpu.VMEM((16, 8, 384), F32),
            pltpu.VMEM((16, 8, 384), F32),
            pltpu.SemaphoreType.DMA((N_SEM,)),
            pltpu.SemaphoreType.DMA((N_SEM,)),
            pltpu.SemaphoreType.DMA((4,)),
            pltpu.SemaphoreType.DMA((6,)),
        ],
        compiler_params=pltpu.CompilerParams(
            collective_id=0, has_side_effects=True, vmem_limit_bytes=56 * 2**20
        ),
        name="soft_moe_backward",
    )(patches, cotangent, other_logsum[:, None, :], slot_keys, w_in, w_out)


def solution(mesh):
    placed = (
        P(("dp", "expert"), None, None),
        P(("dp", "expert"), None, None),
        P(("dp", "expert"), None),
        P(),
        P("expert", None, "dp"),
        P("expert", "dp", None),
    )
    return jax.shard_map(
        on_device,
        mesh=mesh,
        in_specs=placed,
        out_specs=(
            P(("dp", "expert"), None, None),
            P(),
            P("expert", None, "dp"),
            P("expert", "dp", None),
        ),
        check_vma=False,
    )
```

time: 820 us -> 150 us (0.18)
  waiting for transfers between devices: 642 us -> 0 us
  Pallas kernels: 0 us -> 137 us
  blocking collectives: 69.2 us -> 0 us
  local copies, waits for them, and re-layouts: 51.9 us -> 12 us
  matrix products: 27.1 us -> 0 us
  between operations: 14.6 us -> 0.65 us
  starting transfers between devices: 11.2 us -> 0 us
    unnamed x5 -> x0, waiting for transfers between devices: 248 us -> none
    psum x1 -> x0, waiting for transfers between devices: 238 us -> none  [on_device(): key_grad = lax.psum(key_local, ('dp', 'expert'))]
    pallas_call x0 -> x1, Pallas kernels: none -> 137 us  [on_device(): pl.pallas_call(kernel, out_shape=(jax.ShapeDtypeStruct((2, 256, D), BF),...]
    all_gather x2 -> x0, waiting for transfers between devices: 126 us -> none  [the longest x1 65.8 us: on_device(): lax.all_gather(slot_grad, 'dp', axis=0, tiled=True)]
    all_to_all x1 -> x0, blocking collectives: 69.2 us -> none  [on_device(): lax.all_to_all(partial_half, 'expert', split_axis=0, concat_axis=2, tiled...]
    all_to_all x2 -> x0, waiting for transfers between devices: 30 us -> none  [the longest x1 30 us: on_device(): lax.all_to_all(collected[0], 'expert', split_axis=1, concat_axis=0, tiled...]
    all_to_all x4 -> x0, local copies, waits for them, and re-layouts: 27.7 us -> none  [the longest x2 22.2 us: on_device(): lax.all_to_all(partial_half, 'expert', split_axis=0, concat_axis=2, tiled...]
    dot_general x14 -> x0, matrix products: 27.1 us -> none  [the longest x1 4.07 us: expert_side(): jnp.einsum('bed,bef->edf', slot_rows, pre_half, preferred_element_type=jn...]
  transfers between devices with their start and end apart: 6 -> 0, of which waited for: 5 -> 0; matrix products, arithmetic and copies ran while one was open for 3% -> 0% of each run, Pallas kernels for 0% -> 0%
where the time goes in v1:
time: 150 us
  Pallas kernels  137 us (91%)
  local copies, waits for them, and re-layouts  12 us (8%)
    pallas_call x1, Pallas kernels, on_device(): pl.pallas_call(kernel, out_shape=(jax.ShapeDtypeStruct((2, 256, D), BF),...  137 us
    unnamed x10, local copies, waits for them, and re-layouts  6.82 us
    pallas_call x1, local copies, waits for them, and re-layouts, on_device(): pl.pallas_call(kernel, out_shape=(jax.ShapeDtypeStruct((2, 256, D), BF),...  3.97 us

profile of v1, /device:TPU:1, one launch (start us, length us, event | category | flops | bytes accessed | tf_op | source)
XLA Modules:
  0.0 149.8 jit_solution(1628506361280901236)
XLA Ops:
  0.6 1.3 broadcast_in_dim.3.ols_ref
  1.9 3.7 %copy.10.win_hbm = bf16[2,1280,320]{2,1,0:T(8,128)(2,1)} copy(bf16[2,1280,320]{1,2,0:T(8,128)(2,1)} %param.10) | data formatting | bytes 3276800 | tf_op args[4]
  5.5 137.1 %soft_moe_backward.1 = (bf16[2,256,1280]{2,1,0:T(8,128)(2,1)}, f32[32,1280]{1,0:T(8,128)}, bf16[2,1280,320]{2,1,0:T(8,128)(2,1)}, bf16[2,320,1280]{2,1,0:T(8,128)(2,1)}) custom-call(bf16[2,256,1280]{2,1,0:T(8,128)(2,1)} %patches_hbm.1, bf16[2,256,1280]{2,1,0:T(8,128)(2,1)} %cot_hbm.1, f32[2,1,256]{2,1,0:T(1,128)} %broadcast_in_dim.3.ols_ref, ...), custom_call_target="tpu_custom_call" | custom-call | tf_op jit(solution)/shard_map/soft_moe_backward/pallas_call | solution.py:436
  142.7 0.0 copy-start.1
  142.7 4.0 %copy.11 = bf16[2,1280,320]{1,2,0:T(8,128)(2,1)} copy(bf16[2,1280,320]{2,1,0:T(8,128)(2,1)} %get-tuple-element.6) | data formatting | bytes 3276800 | tf_op jit(solution)/shard_map/soft_moe_backward/pallas_call | solution.py:436
  146.6 0.0 copy-done.1
  146.6 0.0 copy-start.2
  146.6 0.0 copy-start
  146.7 1.1 copy.15
  147.7 0.0 copy-done.2
  147.7 0.7 copy.16
  148.4 0.3 copy-done
  148.6 1.2 copy.17
Async XLA Ops:
  142.7 4.0 %copy-start.1 = (bf16[2,256,1280]{2,1,0:T(8,128)(2,1)S(1)}, bf16[2,256,1280]{2,1,0:T(8,128)(2,1)}, u32[]{:S(2)}) copy-start(bf16[2,256,1280]{2,1,0:T(8,128)(2,1)} %get-tuple-element.12) | copy-start | bytes 3932164
  146.6 1.1 copy-start.2
  146.6 2.0 %copy-start = (bf16[2,320,1280]{2,1,0:T(8,128)(2,1)S(1)}, bf16[2,320,1280]{2,1,0:T(8,128)(2,1)}, u32[]{:S(2)}) copy-start(bf16[2,320,1280]{2,1,0:T(8,128)(2,1)} %get-tuple-element.15) | copy-start | bytes 4915204

commit v2 on v1

v2 whole, which is shorter than its diff:
```python
import functools

import jax
import jax.numpy as jnp
from jax import lax
from jax.experimental import pallas as pl
from jax.experimental.pallas import tpu as pltpu
from jax.sharding import PartitionSpec as P

MESH = pl.DeviceIdType.MESH
BF = jnp.bfloat16
F32 = jnp.float32

D = 1280
FB = 320
SPLIT = 1024
COLS = {"A": (0, SPLIT), "B": (SPLIT, D - SPLIT)}
N_RECV = 80
N_SEND = 10
KEY_COLS = (0, 384, 768, 1024)
GELU_C = 0.7978845608028654
GELU_A = 0.044715

ORDER = (
    ("ag1", "A", 0), ("ag1", "B", 0), ("ag2", "A", 1, 0), ("ag2", "A", 0, 0), ("ag2", "B", 0, 0), ("ag1", "B", 1),
    ("ag1", "A", 1), ("ag1_relay", "B", 0), ("ag2_relay", "A", 1, 0), ("ag2", "B", 0, 3), ("ag2_relay", "A", 0, 0),
    ("ag1_relay", "B", 1), ("ag1_relay", "A", 0), ("ag2", "A", 0, 1), ("ag2", "A", 0, 3), ("ag2_relay", "B", 0, 0),
    ("ag2", "B", 0, 1), ("ag2", "B", 0, 2), ("ag2", "B", 1, 1), ("ag2_relay", "A", 0, 1), ("ag2_relay", "B", 0, 3),
    ("ag2", "B", 1, 0), ("ag2_relay", "A", 0, 3), ("ag1_relay", "A", 1), ("ag2", "A", 0, 2), ("ag2", "A", 1, 1),
    ("expert", 0, 0), ("ag2_relay", "B", 0, 1), ("ag2", "A", 1, 3), ("ag2", "B", 1, 2), ("ag2_relay", "B", 0, 2),
    ("ag2_relay", "B", 1, 1), ("ag2_relay", "A", 0, 2), ("expert", 0, 3), ("ag2_relay", "B", 1, 0),
    ("ag2", "B", 1, 3), ("ag2_relay", "A", 1, 1), ("ag2", "A", 1, 2), ("expert", 0, 1), ("rs1_u", "A", 0, 1),
    ("ag2_relay", "B", 1, 2), ("rs1_u", "A", 0, 0), ("ag2_relay", "A", 1, 3), ("expert", 0, 2),
    ("rs1_t", "A", 0, 2), ("ag2_relay", "B", 1, 3), ("rs1_t", "A", 0, 1), ("rs1_t", "B", 0), ("rs1_u", "B", 0),
    ("expert", 1, 0), ("ag2_relay", "A", 1, 2), ("expert", 1, 1), ("rs1_u", "A", 0, 2), ("rs1_t", "A", 0, 3),
    ("expert", 1, 3), ("rs1_m", "B", 0), ("rs1_m", "A", 0, 1), ("rs1_m", "A", 0, 2), ("expert", 1, 2),
    ("rs1_t", "B", 1), ("rs1_t", "A", 1, 2), ("rs1_m", "A", 0, 3), ("rs1_f", "A", 0, 1), ("rs1_u", "B", 1),
    ("rs1_t", "A", 1, 1), ("rs1_u", "A", 0, 3), ("rs1_t", "A", 1, 3), ("rs1_f", "B", 0), ("rs1_f", "A", 0, 2),
    ("rs2_u", "B", 0), ("rs2_t", "A", 0), ("rs1_u", "A", 1, 3), ("weight_grads", 0), ("rs1_m", "B", 1),
    ("rs1_m", "A", 1, 2), ("rs1_m", "A", 1, 1), ("rs1_u", "A", 1, 2), ("rs1_u", "A", 1, 1), ("rs1_f", "A", 0, 3),
    ("rs2_u", "A", 0), ("weight_grads", 1), ("rs2_m", "A", 0), ("rs1_m", "A", 1, 3), ("rs1_f", "B", 1),
    ("rs2_t", "B", 1), ("rs2_u", "B", 1), ("rs1_t", "A", 1, 0), ("rs2_t", "B", 0), ("rs1_f", "A", 1, 2),
    ("rs1_u", "A", 1, 0), ("rs2_t", "A", 1), ("rs1_t", "A", 0, 0), ("rs1_f", "A", 1, 1), ("rs1_f", "A", 1, 3),
    ("rs2_m", "B", 1), ("rs2_u", "A", 1), ("rs1_m", "A", 1, 0), ("rs2_m", "B", 0), ("rs2_m", "A", 1),
    ("rs1_m", "A", 0, 0), ("rs2_f", "B", 1), ("rs1_f", "A", 1, 0), ("rs2_f", "B", 0), ("rs1_f", "A", 0, 0),
    ("rs2_f", "A", 0), ("rs2_f", "A", 1),
)


def dot(a, b):
    return lax.dot_general(a, b, (((1,), (0,)), ((), ())), preferred_element_type=F32)


def dot_nt(a, b):
    return lax.dot_general(a, b, (((1,), (1,)), ((), ())), preferred_element_type=F32)


def dot_tn(a, b):
    return lax.dot_general(a, b, (((0,), (0,)), ((), ())), preferred_element_type=F32)


def iota(shape, dim):
    return lax.broadcasted_iota(jnp.int32, shape, dim)


def piece_row(slot_off, half, k, t, i):
    return slot_off * 16 + half * 8 + k * 4 + t * 2 + i


def spread_index(r, me):
    off, k, t, i = r >> 4, (r >> 2) & 1, (r >> 1) & 1, r & 1
    owner = (me + off) & 15
    return (t * 2 + i) * 32 + 2 * owner + k


def block_index(r):
    off, k, t, i = r >> 4, (r >> 2) & 1, (r >> 1) & 1, r & 1
    return (k * 2 + t) * 32 + off * 2 + i


def one_hot(index_of, half, rows_are_pieces):
    shape = (256, 128) if rows_are_pieces else (128, 256)
    piece = iota(shape, 0 if rows_are_pieces else 1)
    other = iota(shape, 1 if rows_are_pieces else 0)
    hit = (index_of(piece) == other) & (((piece >> 3) & 1) == half)
    return jnp.where(hit, 1.0, 0.0).astype(BF)


def kernel(
    patches_hbm, cot_hbm, ols_ref, keys_ref, win_hbm, wout_hbm,
    pg_hbm, kg_ref, wig_hbm, wog_hbm,
    patches, cot, win, wout, pg, wig, wog,
    disp_s, comb_s, g, pt, act_s, pre_s, r1, r2,
    a2s, a2r, b2s, b2r, ks, k1, k2, k3, k4,
    send_sem, recv_sem, in_sem, out_sem,
):
    dp = lax.axis_index("dp")
    me = lax.axis_index("expert")
    zh, y = dp // 4, dp % 4

    def expert_peer(off):
        return (dp, lax.rem(me + off, 16))

    def dp_peer(off):
        return (lax.rem(dp + off, 16), me)

    def ring_peer(axis, step):
        if axis == "y":
            return (zh * 4 + lax.rem(y + step + 4, 4), me)
        return (lax.rem(zh + step + 4, 4) * 4 + y, me)

    barrier = pltpu.get_barrier_semaphore()
    for off in range(1, 16):
        pl.semaphore_signal(barrier, inc=1, device_id=expert_peer(off), device_id_type=MESH)
        pl.semaphore_signal(barrier, inc=1, device_id=dp_peer(off), device_id_type=MESH)

    loads = {}
    for n, (name, src, dst) in enumerate(
        (("x", patches_hbm, patches), ("c", cot_hbm, cot), ("wi", win_hbm, win), ("wo", wout_hbm, wout))
    ):
        loads[name] = pltpu.make_async_copy(src, dst, in_sem.at[n])
    loads["x"].start()
    loads["c"].start()

    recv_of, send_of, waited = {}, {}, set()

    def send(group, out, src, dst, device):
        n = recv_of.setdefault(group, len(recv_of))
        m = send_of.setdefault(out, len(send_of))
        assert n < N_RECV and m < N_SEND
        pltpu.make_async_remote_copy(
            src_ref=src, dst_ref=dst, send_sem=send_sem.at[m], recv_sem=recv_sem.at[n],
            device_id=device, device_id_type=MESH,
        ).start()

    def total_of(ref, n, m):
        return pltpu.make_async_remote_copy(
            src_ref=ref, dst_ref=ref, send_sem=send_sem.at[m], recv_sem=recv_sem.at[n],
            device_id=expert_peer(1), device_id_type=MESH,
        )

    def got(group, ref):
        if group not in waited:
            waited.add(group)
            total_of(ref, recv_of[group], 0).wait_recv()

    def sent(out, ref):
        total_of(ref, 0, send_of.pop(out)).wait_send()

    keys = keys_ref[...]
    loads["x"].wait()
    loads["c"].wait()
    loads["wi"].start()
    loads["wo"].start()
    rows_in, rows_grad = [], []
    for i in range(2):
        exponent = jnp.exp(dot_nt(keys, patches[i]))
        dispatch = exponent / jnp.sum(exponent, axis=1, keepdims=True)
        combine = exponent / (jnp.sum(exponent, axis=0, keepdims=True) + jnp.exp(ols_ref[i : i + 1, :]))
        disp_s[i] = dispatch
        comb_s[i] = combine
        rows_in.append(dot(dispatch.astype(BF), patches[i]).astype(BF))
        rows_grad.append(dot(combine.astype(BF), cot[i]).astype(BF))
    rows = jnp.concatenate(rows_in + rows_grad, axis=0)

    def to_pieces(rows, index_of, dst):
        half = D // 2
        pieces = dot(one_hot(index_of, 0, True), rows[:, :half]) + dot(
            one_hot(index_of, 1, True), rows[:, half:]
        )
        dst[...] = pieces.astype(BF).reshape(16, 16, half)

    def from_pieces(src, index_of, half):
        pieces = src[...].reshape(256, D // 2)
        return dot(one_hot(index_of, half, False), pieces).astype(BF)

    spread = functools.partial(spread_index, me=me)
    to_pieces(rows, spread, a2s)
    a2r[0] = a2s[0]
    pl.semaphore_wait(barrier, 30)
    for off in range(1, 16):
        send("a", "a", a2s.at[off], a2r.at[off], expert_peer(off))
    got("a", a2r.at[pl.ds(1, 15)])
    for half in range(2):
        cols = slice(half * 640, half * 640 + 640)
        g[:, 0, 0, :, cols] = from_pieces(a2r, block_index, half).reshape(4, 32, 640)

    AXES = {"A": ("z", "y"), "B": ("y", "z")}

    def cols_of(part):
        return pl.ds(*COLS[part])

    def at(ref, part, k, a1, a2, r0=0, nr=32):
        dy, dz = (a2, a1) if part == "A" else (a1, a2)
        return ref.at[pl.ds(2 * k, 2), dy, dz, pl.ds(r0, nr), cols_of(part)]

    def two(part, k):
        return g.at[pl.ds(2 * k, 2), 0, pl.ds(0, 2), :, cols_of(part)]

    def ag1(part, k):
        for step, a in ((1, 3), (-1, 1)):
            send(("p1", part, k), "ag1", at(g, part, k, 0, 0), at(g, part, k, a, 0), ring_peer(AXES[part][0], step))

    def ag1_relay(part, k):
        got(("p1", part, k), two(part, k))
        for step, a, r in ((1, 3, 0), (-1, 1, 16)):
            send(("r1", part, k), "ag1", at(g, part, k, a, 0, r, 16), at(g, part, k, 2, 0, r, 16), ring_peer(AXES[part][0], step))

    def first_in(part, k, a1):
        if a1 in (1, 3):
            got(("p1", part, k), two(part, k))
        if a1 == 2:
            got(("r1", part, k), at(g, part, k, 2, 0))

    def ag2(part, k, a1):
        first_in(part, k, a1)
        for step, a in ((1, 3), (-1, 1)):
            send(("p2", part, k, a1), "ag2", at(g, part, k, a1, 0), at(g, part, k, a1, a), ring_peer(AXES[part][1], step))

    def ag2_relay(part, k, a1):
        got(("p2", part, k, a1), two(part, k))
        for step, a, r in ((1, 3, 0), (-1, 1, 16)):
            send(("r2", part, k, a1), "ag2", at(g, part, k, a1, a, r, 16), at(g, part, k, a1, 2, r, 16), ring_peer(AXES[part][1], step))

    def slot_in(part, k, a1, a2):
        if a2 == 0:
            first_in(part, k, a1)
        elif a2 == 2:
            got(("r2", part, k, a1), at(g, part, k, a1, 2))
        else:
            got(("p2", part, k, a1), two(part, k))

    def expert(k, dy):
        for n in range(4):
            slot_in("A", k, n, dy)
            slot_in("B", k, dy, n)
        if "w" not in waited:
            waited.add("w")
            loads["wi"].wait()
            loads["wo"].wait()
        x0 = g[2 * k, dy].reshape(128, D)
        x1 = g[2 * k + 1, dy].reshape(128, D)
        hidden = dot_nt(x0, win[k])
        upstream = dot_nt(x1, wout[k])
        square = hidden * hidden
        tanh = jnp.tanh(GELU_C * (hidden + GELU_A * square * hidden))
        act = (0.5 * hidden * (1.0 + tanh)).astype(BF)
        slope = 0.5 * (1.0 + tanh) + (0.5 * hidden) * (1.0 - tanh * tanh) * (
            GELU_C + (3.0 * GELU_C * GELU_A) * square
        )
        pre = (slope * upstream).astype(BF)
        act_s[k, dy * 128 : dy * 128 + 128, :] = act
        pre_s[k, dy * 128 : dy * 128 + 128, :] = pre
        pt[2 * k, dy] = dot(act, wout[k]).astype(BF).reshape(4, 32, D)
        pt[2 * k + 1, dy] = dot(pre, win[k]).astype(BF).reshape(4, 32, D)

    def weight_grads(k):
        wog[k] = dot_tn(act_s[k], g[2 * k + 1].reshape(512, D)).astype(BF)
        wig[k] = dot_tn(pre_s[k], g[2 * k].reshape(512, D)).astype(BF)
        for n, (src, dst) in enumerate(((wig, wig_hbm), (wog, wog_hbm))):
            stores.append(pltpu.make_async_copy(src.at[k], dst.at[k], out_sem.at[2 * k + n]))
            stores[-1].start()

    stores = []

    TP, TM, UP, MP, UM, MM = range(6)

    def part_of(ph, part, k, a1, a2, r0):
        if ph == 1 and part == "B":
            return pt.at[pl.ds(2 * k, 2), :, a2, pl.ds(r0, 16), cols_of(part)]
        if ph == 1:
            return at(pt, part, k, a1, a2, r0, 16)
        return at(pt, part, k, a2, 0, r0, 16)

    def land(ph, part, k, a1, m):
        if ph == 1:
            return r1.at[k, m, :, slice(None) if part == "B" else a1, :, cols_of(part)]
        return r2.at[k, m, :, :, cols_of(part)]

    def rs_send(ph, part, k, a1, m, a2, r0):
        step = 1 if m in (TP, UP, MP) else -1
        kind = "t" if m < 2 else "u"
        send((kind, ph, part, k, a1), ("rs", ph), part_of(ph, part, k, a1, a2, r0), land(ph, part, k, a1, m), ring_peer(AXES[part][2 - ph], step))

    def rs_got(ph, part, k, a1, kind):
        m = pl.ds(0, 2) if kind == "t" else pl.ds(2, 4)
        got((kind, ph, part, k, a1), land(ph, part, k, a1, m))

    def rs_t(ph, part, k, a1=None):
        rs_send(ph, part, k, a1, TP, 2, 16)
        rs_send(ph, part, k, a1, TM, 2, 0)

    def rs_u(ph, part, k, a1=None):
        rs_send(ph, part, k, a1, UP, 1, 0)
        rs_send(ph, part, k, a1, UM, 3, 16)

    def add_into(dst, *srcs):
        total = dst[...].astype(F32)
        for src in srcs:
            total = total + src[...].astype(F32)
        dst[...] = total.astype(BF)

    def rs_m(ph, part, k, a1=None):
        rs_got(ph, part, k, a1, "t")
        for t, m, a2, r0 in ((TP, MP, 1, 16), (TM, MM, 3, 0)):
            add_into(part_of(ph, part, k, a1, a2, r0), land(ph, part, k, a1, t))
            rs_send(ph, part, k, a1, m, a2, r0)

    def rs_f(ph, part, k, a1=None):
        rs_got(ph, part, k, a1, "u")
        for u, m, r0 in ((UP, MM, 0), (UM, MP, 16)):
            add_into(part_of(ph, part, k, a1, 0, r0), land(ph, part, k, a1, u), land(ph, part, k, a1, m))

    steps = {"ag1": ag1, "ag1_relay": ag1_relay, "ag2": ag2, "ag2_relay": ag2_relay, "expert": expert, "weight_grads": weight_grads}
    for ph in (1, 2):
        for name, step in (("t", rs_t), ("u", rs_u), ("m", rs_m), ("f", rs_f)):
            steps["rs%d_%s" % (ph, name)] = functools.partial(step, ph)
    for name, *where in ORDER:
        steps[name](*where)

    to_pieces(pt[:, 0, 0].reshape(128, D), block_index, b2s)
    b2r[0] = b2s[0]
    for off in range(1, 16):
        send("b", "b", b2s.at[off], b2r.at[off], expert_peer(16 - off))
    got("b", b2r.at[pl.ds(1, 15)])
    back = jnp.concatenate([from_pieces(b2r, spread, half) for half in range(2)], axis=1)

    halves = []
    key_part = jnp.zeros((32, D), F32)
    for i in range(2):
        slot_out = back[i * 32 : i * 32 + 32]
        slot_in_grad = back[64 + i * 32 : 96 + i * 32]
        comb_grad = dot_nt(slot_out, cot[i])
        disp_grad = dot_nt(slot_in_grad, patches[i])
        dispatch = disp_s[i]
        combine = comb_s[i]
        logit_grad = combine * (comb_grad - jnp.sum(combine * comb_grad, axis=0, keepdims=True))
        logit_grad = logit_grad + dispatch * (
            disp_grad - jnp.sum(dispatch * disp_grad, axis=1, keepdims=True)
        )
        logit_half = logit_grad.astype(BF)
        key_part = key_part + dot(logit_half, patches[i])
        halves.append((dispatch.astype(BF), logit_half, slot_in_grad))

    for o in range(16):
        rg, c0 = (o // 4) * 8, KEY_COLS[o % 4]
        top = key_part[rg : rg + 8, c0 : c0 + 256]
        low = jnp.zeros((8, 256), F32)
        if o % 4 < 2:
            low = jnp.concatenate([key_part[rg : rg + 8, c0 + 256 : c0 + 384], low[:, :128]], axis=1)
        ks[o] = jnp.concatenate([top, low], axis=0).astype(BF)
    for off in range(1, 16):
        send("k1", "k1", ks.at[lax.rem(me + off, 16)], k1.at[off], expert_peer(off))

    def image_out(i):
        dispatch_half, logit_half, slot_in_grad = halves[i]
        lhs = jnp.concatenate([dispatch_half, logit_half], axis=0)
        rhs = jnp.concatenate([slot_in_grad, keys], axis=0)
        pg[i] = dot_tn(lhs, rhs).astype(BF)
        stores.append(pltpu.make_async_copy(pg.at[i], pg_hbm.at[i], out_sem.at[4 + i]))
        stores[-1].start()

    image_out(0)
    total = ks[me].astype(F32)
    got("k1", k1.at[pl.ds(1, 15)])
    for off in range(1, 16):
        total = total + k1[off].astype(F32)
    k2[0] = total.astype(BF)
    for off in range(1, 16):
        send("k2", "k2", k2.at[0], k2.at[off], dp_peer(off))
    image_out(1)
    got("k2", k2.at[pl.ds(1, 15)])
    total = k2[lax.rem(dp, 16)].astype(F32)
    for n in range(1, 16):
        total = total + k2[lax.rem(dp + 16 - n, 16)].astype(F32)
    k3[0] = total.astype(BF)
    for off in range(1, 16):
        send("k3", "k3", k3.at[0], k3.at[off], expert_peer(off))
    k4[me] = k3[0]
    got("k3", k3.at[pl.ds(1, 15)])
    for off in range(1, 16):
        k4[lax.rem(me + 16 - off, 16)] = k3[off]
    for o in range(16):
        rg, c0 = (o // 4) * 8, KEY_COLS[o % 4]
        piece = k4[o].astype(F32)
        kg_ref[rg : rg + 8, c0 : c0 + 256] = piece[:8]
        if o % 4 < 2:
            kg_ref[rg : rg + 8, c0 + 256 : c0 + 384] = piece[8:, :128]
    for store in stores:
        store.wait()
    for out, ref in (("a", a2s), ("b", b2s), ("k1", k1), ("k2", k2), ("k3", k3)):
        sent(out, ref.at[pl.ds(1, 15)])
    sent("ag1", g.at[:, 0, pl.ds(1, 3)])
    sent("ag2", g.at[:, pl.ds(1, 3)])
    sent(("rs", 1), r1)
    sent(("rs", 2), r2)
    assert not send_of and len(waited) == len(recv_of) + 1


def on_device(patches, cotangent, other_logsum, slot_keys, w_in, w_out):
    any_spec = pl.BlockSpec(memory_space=pl.ANY)
    vmem = pl.BlockSpec(memory_space=pltpu.VMEM)
    patch_grad, key_grad, w_in_grad, w_out_grad = pl.pallas_call(
        kernel,
        out_shape=(
            jax.ShapeDtypeStruct((2, 256, D), BF),
            jax.ShapeDtypeStruct((32, D), F32),
            jax.ShapeDtypeStruct((2, FB, D), BF),
            jax.ShapeDtypeStruct((2, FB, D), BF),
        ),
        in_specs=[any_spec, any_spec, vmem, vmem, any_spec, any_spec],
        out_specs=(any_spec, vmem, any_spec, any_spec),
        scratch_shapes=[
            pltpu.VMEM((2, 256, D), BF),
            pltpu.VMEM((2, 256, D), BF),
            pltpu.VMEM((2, FB, D), BF),
            pltpu.VMEM((2, FB, D), BF),
            pltpu.VMEM((2, 256, D), BF),
            pltpu.VMEM((2, FB, D), BF),
            pltpu.VMEM((2, FB, D), BF),
            pltpu.VMEM((2, 32, 256), F32),
            pltpu.VMEM((2, 32, 256), F32),
            pltpu.VMEM((4, 4, 4, 32, D), BF),
            pltpu.VMEM((4, 4, 4, 32, D), BF),
            pltpu.VMEM((2, 512, FB), BF),
            pltpu.VMEM((2, 512, FB), BF),
            pltpu.VMEM((2, 6, 2, 4, 16, D), BF),
            pltpu.VMEM((2, 6, 2, 16, D), BF),
            pltpu.VMEM((16, 16, D // 2), BF),
            pltpu.VMEM((16, 16, D // 2), BF),
            pltpu.VMEM((16, 16, D // 2), BF),
            pltpu.VMEM((16, 16, D // 2), BF),
            pltpu.VMEM((16, 16, 256), BF),
            pltpu.VMEM((16, 16, 256), BF),
            pltpu.VMEM((16, 16, 256), BF),
            pltpu.VMEM((16, 16, 256), BF),
            pltpu.VMEM((16, 16, 256), BF),
            pltpu.SemaphoreType.DMA((N_SEND,)),
            pltpu.SemaphoreType.DMA((N_RECV,)),
            pltpu.SemaphoreType.DMA((4,)),
            pltpu.SemaphoreType.DMA((6,)),
        ],
        compiler_params=pltpu.CompilerParams(
            collective_id=0, has_side_effects=True, vmem_limit_bytes=56 * 2**20
        ),
        name="soft_moe_backward",
    )(patches, cotangent, other_logsum, slot_keys, jnp.swapaxes(w_in, 1, 2), w_out)
    return (patch_grad, key_grad, jnp.swapaxes(w_in_grad, 1, 2), w_out_grad)


def solution(mesh):
    placed = (
        P(("dp", "expert"), None, None),
        P(("dp", "expert"), None, None),
        P(("dp", "expert"), None),
        P(),
        P("expert", None, "dp"),
        P("expert", "dp", None),
    )
    return jax.shard_map(
        on_device,
        mesh=mesh,
        in_specs=placed,
        out_specs=(
            P(("dp", "expert"), None, None),
            P(),
            P("expert", None, "dp"),
            P("expert", "dp", None),
        ),
        check_vma=False,
    )
```

time: 150 us -> 128 us (0.85)
  Pallas kernels: 137 us -> 121 us
  local copies, waits for them, and re-layouts: 12 us -> 6.45 us
    pallas_call x1, Pallas kernels: 137 us -> 121 us  [on_device(): pl.pallas_call(kernel, out_shape=(jax.ShapeDtypeStruct((2, 256, D), BF),...]
    pallas_call x1 -> x0, local copies, waits for them, and re-layouts: 3.97 us -> none  [on_device(): pl.pallas_call(kernel, out_shape=(jax.ShapeDtypeStruct((2, 256, D), BF),...]
where the time goes in v2:
time: 128 us
  Pallas kernels  121 us (95%)
  local copies, waits for them, and re-layouts  6.45 us (5%)
    pallas_call x1, Pallas kernels, on_device(): pl.pallas_call(kernel, out_shape=(jax.ShapeDtypeStruct((2, 256, D), BF),...  121 us
    unnamed x10, local copies, waits for them, and re-layouts  6.45 us

profile of v2, /device:TPU:1, one launch (start us, length us, event | category | flops | bytes accessed | tf_op | source)
XLA Modules:
  0.0 128.0 jit_solution(12572537908335059051)
XLA Ops:
  0.6 120.8 %soft_moe_backward.1 = (bf16[2,256,1280]{2,1,0:T(8,128)(2,1)}, f32[32,1280]{1,0:T(8,128)}, bf16[2,320,1280]{2,1,0:T(8,128)(2,1)}, bf16[2,320,1280]{2,1,0:T(8,128)(2,1)}) custom-call(bf16[2,256,1280]{2,1,0:T(8,128)(2,1)} %patches_hbm.1, bf16[2,256,1280]{2,1,0:T(8,128)(2,1)} %cot_hbm.1, f32[2,256]{1,0:T(2,128)} %ols_ref.1, bf16[32,1280]{1,0:T(8,128)(2,1)} %keys_ref.1, ...), custom_call_target="tpu_custom_call" | custom-call | tf_op jit(solution)/shard_map/soft_moe_backward/pallas_call | solution.py:403
  121.5 0.0 copy-start.2
  121.5 0.0 copy-start.1
  121.5 2.6 %copy.14 = bf16[2,256,1280]{2,1,0:T(8,128)(2,1)} copy(bf16[2,256,1280]{2,1,0:T(8,128)(2,1)} %get-tuple-element.16) | data formatting | bytes 2621440
  124.1 0.0 copy-done.2
  124.1 0.7 copy.15
  124.8 0.0 copy-done.1
  124.8 0.0 copy-start
  124.8 1.2 copy.16
  125.9 0.9 copy-done
  126.8 1.2 copy.17
Async XLA Ops:
  121.5 2.6 %copy-start.2 = (f32[32,1280]{1,0:T(8,128)S(1)}, f32[32,1280]{1,0:T(8,128)}, u32[]{:S(2)}) copy-start(f32[32,1280]{1,0:T(8,128)} %get-tuple-element.17) | copy-start | bytes 491524
  121.5 3.3 %copy-start.1 = (bf16[2,320,1280]{2,1,0:T(8,128)(2,1)S(1)}, bf16[2,320,1280]{2,1,0:T(8,128)(2,1)}, u32[]{:S(2)}) copy-start(bf16[2,320,1280]{2,1,0:T(8,128)(2,1)} %get-tuple-element.10) | copy-start | bytes 4915204
  124.8 2.0 %copy-start = (bf16[2,320,1280]{2,1,0:T(8,128)(2,1)S(1)}, bf16[2,320,1280]{2,1,0:T(8,128)(2,1)}, u32[]{:S(2)}) copy-start(bf16[2,320,1280]{2,1,0:T(8,128)(2,1)} %get-tuple-element.19) | copy-start | bytes 4915204

commit v3 on v2

--- a/solution.py
+++ b/solution.py
@@ -17,33 +17,33 @@
 COLS = {"A": (0, SPLIT), "B": (SPLIT, D - SPLIT)}
 N_RECV = 80
 N_SEND = 10
-KEY_COLS = (0, 384, 768, 1024)
+OWNERS = 10
 GELU_C = 0.7978845608028654
 GELU_A = 0.044715
 
 ORDER = (
-    ("ag1", "A", 0), ("ag1", "B", 0), ("ag2", "A", 1, 0), ("ag2", "A", 0, 0), ("ag2", "B", 0, 0), ("ag1", "B", 1),
-    ("ag1", "A", 1), ("ag1_relay", "B", 0), ("ag2_relay", "A", 1, 0), ("ag2", "B", 0, 3), ("ag2_relay", "A", 0, 0),
-    ("ag1_relay", "B", 1), ("ag1_relay", "A", 0), ("ag2", "A", 0, 1), ("ag2", "A", 0, 3), ("ag2_relay", "B", 0, 0),
-    ("ag2", "B", 0, 1), ("ag2", "B", 0, 2), ("ag2", "B", 1, 1), ("ag2_relay", "A", 0, 1), ("ag2_relay", "B", 0, 3),
-    ("ag2", "B", 1, 0), ("ag2_relay", "A", 0, 3), ("ag1_relay", "A", 1), ("ag2", "A", 0, 2), ("ag2", "A", 1, 1),
-    ("expert", 0, 0), ("ag2_relay", "B", 0, 1), ("ag2", "A", 1, 3), ("ag2", "B", 1, 2), ("ag2_relay", "B", 0, 2),
-    ("ag2_relay", "B", 1, 1), ("ag2_relay", "A", 0, 2), ("expert", 0, 3), ("ag2_relay", "B", 1, 0),
-    ("ag2", "B", 1, 3), ("ag2_relay", "A", 1, 1), ("ag2", "A", 1, 2), ("expert", 0, 1), ("rs1_u", "A", 0, 1),
-    ("ag2_relay", "B", 1, 2), ("rs1_u", "A", 0, 0), ("ag2_relay", "A", 1, 3), ("expert", 0, 2),
-    ("rs1_t", "A", 0, 2), ("ag2_relay", "B", 1, 3), ("rs1_t", "A", 0, 1), ("rs1_t", "B", 0), ("rs1_u", "B", 0),
-    ("expert", 1, 0), ("ag2_relay", "A", 1, 2), ("expert", 1, 1), ("rs1_u", "A", 0, 2), ("rs1_t", "A", 0, 3),
-    ("expert", 1, 3), ("rs1_m", "B", 0), ("rs1_m", "A", 0, 1), ("rs1_m", "A", 0, 2), ("expert", 1, 2),
-    ("rs1_t", "B", 1), ("rs1_t", "A", 1, 2), ("rs1_m", "A", 0, 3), ("rs1_f", "A", 0, 1), ("rs1_u", "B", 1),
-    ("rs1_t", "A", 1, 1), ("rs1_u", "A", 0, 3), ("rs1_t", "A", 1, 3), ("rs1_f", "B", 0), ("rs1_f", "A", 0, 2),
-    ("rs2_u", "B", 0), ("rs2_t", "A", 0), ("rs1_u", "A", 1, 3), ("weight_grads", 0), ("rs1_m", "B", 1),
-    ("rs1_m", "A", 1, 2), ("rs1_m", "A", 1, 1), ("rs1_u", "A", 1, 2), ("rs1_u", "A", 1, 1), ("rs1_f", "A", 0, 3),
-    ("rs2_u", "A", 0), ("weight_grads", 1), ("rs2_m", "A", 0), ("rs1_m", "A", 1, 3), ("rs1_f", "B", 1),
-    ("rs2_t", "B", 1), ("rs2_u", "B", 1), ("rs1_t", "A", 1, 0), ("rs2_t", "B", 0), ("rs1_f", "A", 1, 2),
-    ("rs1_u", "A", 1, 0), ("rs2_t", "A", 1), ("rs1_t", "A", 0, 0), ("rs1_f", "A", 1, 1), ("rs1_f", "A", 1, 3),
-    ("rs2_m", "B", 1), ("rs2_u", "A", 1), ("rs1_m", "A", 1, 0), ("rs2_m", "B", 0), ("rs2_m", "A", 1),
-    ("rs1_m", "A", 0, 0), ("rs2_f", "B", 1), ("rs1_f", "A", 1, 0), ("rs2_f", "B", 0), ("rs1_f", "A", 0, 0),
-    ("rs2_f", "A", 0), ("rs2_f", "A", 1),
+    ("ag2", "A", 1, 0), ("ag1", "B", 0), ("ag1", "A", 0), ("ag2", "B", 0, 0), ("ag2", "A", 0, 0), ("ag1", "B", 1),
+    ("ag1", "A", 1), ("ag2_relay", "A", 1, 0), ("ag1_relay", "B", 0), ("ag2", "B", 0, 1), ("ag2_relay", "A", 0, 0),
+    ("ag2", "B", 0, 3), ("ag1_relay", "B", 1), ("ag1_relay", "A", 0), ("ag2", "A", 0, 1), ("ag2", "A", 0, 3),
+    ("ag2_relay", "B", 0, 0), ("ag2", "B", 1, 3), ("ag2", "B", 1, 0), ("ag2_relay", "A", 0, 1),
+    ("ag1_relay", "A", 1), ("ag2", "A", 1, 1), ("ag2", "A", 1, 3), ("ag2_relay", "A", 0, 3),
+    ("ag2_relay", "B", 0, 3), ("ag2_relay", "B", 0, 1), ("ag2", "B", 0, 2), ("ag2", "A", 0, 2), ("ag2", "B", 1, 2),
+    ("expert", 0, 0), ("ag2_relay", "A", 1, 1), ("ag2_relay", "B", 1, 3), ("ag2", "B", 1, 1),
+    ("ag2_relay", "A", 1, 3), ("ag2_relay", "B", 1, 0), ("ag2", "A", 1, 2), ("ag2_relay", "A", 0, 2),
+    ("expert", 0, 1), ("ag2_relay", "B", 0, 2), ("expert", 0, 3), ("rs1_u", "A", 0, 1), ("rs1_u", "A", 0, 2),
+    ("ag2_relay", "B", 1, 1), ("ag2_relay", "B", 1, 2), ("rs1_u", "A", 0, 0), ("rs1_u", "A", 0, 3),
+    ("expert", 1, 0), ("ag2_relay", "A", 1, 2), ("expert", 0, 2), ("rs1_t", "A", 0, 2), ("rs1_t", "B", 0),
+    ("expert", 1, 1), ("rs1_t", "A", 0, 1), ("rs1_u", "B", 0), ("rs1_t", "A", 0, 3), ("expert", 1, 3),
+    ("rs1_u", "A", 1, 2), ("rs1_u", "A", 1, 3), ("expert", 1, 2), ("rs1_u", "B", 1), ("rs1_m", "A", 0, 2),
+    ("rs1_t", "A", 1, 2), ("rs1_t", "B", 1), ("rs1_t", "A", 1, 3), ("rs1_m", "B", 0), ("rs1_t", "A", 1, 1),
+    ("weight_grads", 1), ("rs1_m", "A", 0, 3), ("rs1_m", "A", 0, 1), ("rs1_f", "A", 0, 2), ("rs2_t", "A", 0),
+    ("rs1_u", "A", 1, 0), ("weight_grads", 0), ("rs1_m", "B", 1), ("rs1_f", "B", 0), ("rs2_t", "B", 0),
+    ("rs1_m", "A", 1, 1), ("rs1_f", "A", 0, 3), ("rs1_m", "A", 1, 3), ("rs1_m", "A", 1, 2), ("rs1_f", "A", 0, 1),
+    ("rs2_u", "A", 0), ("rs1_u", "A", 1, 1), ("rs2_u", "B", 0), ("rs2_m", "A", 0), ("rs1_t", "A", 0, 0),
+    ("rs1_t", "A", 1, 0), ("rs2_m", "B", 0), ("rs1_f", "B", 1), ("rs2_t", "B", 1), ("rs2_u", "B", 1),
+    ("rs1_f", "A", 1, 3), ("rs1_f", "A", 1, 2), ("rs2_t", "A", 1), ("rs1_f", "A", 1, 1), ("rs2_u", "A", 1),
+    ("rs1_m", "A", 0, 0), ("rs1_m", "A", 1, 0), ("rs2_f", "B", 0), ("rs2_m", "B", 1), ("rs2_m", "A", 1),
+    ("rs1_f", "A", 0, 0), ("rs2_f", "A", 0), ("rs1_f", "A", 1, 0), ("rs2_f", "B", 1), ("rs2_f", "A", 1),
 )
 
 
@@ -88,11 +88,11 @@
 
 def kernel(
     patches_hbm, cot_hbm, ols_ref, keys_ref, win_hbm, wout_hbm,
-    pg_hbm, kg_ref, wig_hbm, wog_hbm,
-    patches, cot, win, wout, pg, wig, wog,
+    pg, kg_ref, wig, wog,
+    patches, cot, win, wout,
     disp_s, comb_s, g, pt, act_s, pre_s, r1, r2,
-    a2s, a2r, b2s, b2r, ks, k1, k2, k3, k4,
-    send_sem, recv_sem, in_sem, out_sem,
+    a2s, a2r, b2s, b2r, ks, k1, k2, k3,
+    send_sem, recv_sem, in_sem,
 ):
     dp = lax.axis_index("dp")
     me = lax.axis_index("expert")
@@ -257,11 +257,6 @@
     def weight_grads(k):
         wog[k] = dot_tn(act_s[k], g[2 * k + 1].reshape(512, D)).astype(BF)
         wig[k] = dot_tn(pre_s[k], g[2 * k].reshape(512, D)).astype(BF)
-        for n, (src, dst) in enumerate(((wig, wig_hbm), (wog, wog_hbm))):
-            stores.append(pltpu.make_async_copy(src.at[k], dst.at[k], out_sem.at[2 * k + n]))
-            stores[-1].start()
-
-    stores = []
 
     TP, TM, UP, MP, UM, MM = range(6)
 
@@ -342,53 +337,73 @@
         key_part = key_part + dot(logit_half, patches[i])
         halves.append((dispatch.astype(BF), logit_half, slot_in_grad))
 
-    for o in range(16):
-        rg, c0 = (o // 4) * 8, KEY_COLS[o % 4]
-        top = key_part[rg : rg + 8, c0 : c0 + 256]
-        low = jnp.zeros((8, 256), F32)
-        if o % 4 < 2:
-            low = jnp.concatenate([key_part[rg : rg + 8, c0 + 256 : c0 + 384], low[:, :128]], axis=1)
-        ks[o] = jnp.concatenate([top, low], axis=0).astype(BF)
-    for off in range(1, 16):
-        send("k1", "k1", ks.at[lax.rem(me + off, 16)], k1.at[off], expert_peer(off))
+    def piece(o):
+        return slice(o // 5 * 16, o // 5 * 16 + 16), slice(o % 5 * 256, o % 5 * 256 + 256)
+
+    owner = me < OWNERS
+    for o in range(OWNERS):
+        ks[o] = key_part[piece(o)].astype(BF)
+
+        @pl.when(me != o)
+        def _():
+            send("k1", "k1", ks.at[o], k1.at[me], (dp, o))
 
     def image_out(i):
         dispatch_half, logit_half, slot_in_grad = halves[i]
         lhs = jnp.concatenate([dispatch_half, logit_half], axis=0)
         rhs = jnp.concatenate([slot_in_grad, keys], axis=0)
         pg[i] = dot_tn(lhs, rhs).astype(BF)
-        stores.append(pltpu.make_async_copy(pg.at[i], pg_hbm.at[i], out_sem.at[4 + i]))
-        stores[-1].start()
 
     image_out(0)
-    total = ks[me].astype(F32)
-    got("k1", k1.at[pl.ds(1, 15)])
-    for off in range(1, 16):
-        total = total + k1[off].astype(F32)
-    k2[0] = total.astype(BF)
-    for off in range(1, 16):
-        send("k2", "k2", k2.at[0], k2.at[off], dp_peer(off))
+
+    @pl.when(owner)
+    def _():
+        k1[me] = ks[me]
+        got("k1", k1.at[pl.ds(1, 15)])
+        total = k1[0].astype(F32)
+        for n in range(1, 16):
+            total = total + k1[n].astype(F32)
+        k2[dp] = total.astype(BF)
+        for off in range(1, 16):
+            send("k2", "k2", k2.at[dp], k2.at[dp], dp_peer(off))
+
     image_out(1)
-    got("k2", k2.at[pl.ds(1, 15)])
-    total = k2[lax.rem(dp, 16)].astype(F32)
-    for n in range(1, 16):
-        total = total + k2[lax.rem(dp + 16 - n, 16)].astype(F32)
-    k3[0] = total.astype(BF)
-    for off in range(1, 16):
-        send("k3", "k3", k3.at[0], k3.at[off], expert_peer(off))
-    k4[me] = k3[0]
-    got("k3", k3.at[pl.ds(1, 15)])
-    for off in range(1, 16):
-        k4[lax.rem(me + 16 - off, 16)] = k3[off]
-    for o in range(16):
-        rg, c0 = (o // 4) * 8, KEY_COLS[o % 4]
-        piece = k4[o].astype(F32)
-        kg_ref[rg : rg + 8, c0 : c0 + 256] = piece[:8]
-        if o % 4 < 2:
-            kg_ref[rg : rg + 8, c0 + 256 : c0 + 384] = piece[8:, :128]
-    for store in stores:
-        store.wait()
-    for out, ref in (("a", a2s), ("b", b2s), ("k1", k1), ("k2", k2), ("k3", k3)):
+
+    @pl.when(owner)
+    def _():
+        got("k2", k2.at[pl.ds(1, 15)])
+        total = k2[0].astype(F32)
+        for n in range(1, 16):
+            total = total + k2[n].astype(F32)
+        k3[me] = total.astype(BF)
+        for off in range(1, 16):
+            send("k3", "k3", k3.at[me], k3.at[me], expert_peer(off))
+
+    n_k1, n_k3 = send_of["k1"], recv_of["k3"]
+    waited.add("k3")
+
+    @pl.when(owner)
+    def _():
+        total_of(k3.at[pl.ds(0, OWNERS - 1)], n_k3, 0).wait_recv()
+
+    @pl.when(jnp.logical_not(owner))
+    def _():
+        total_of(k3, n_k3, 0).wait_recv()
+
+    for o in range(OWNERS):
+        kg_ref[piece(o)] = k3[o].astype(F32)
+
+    @pl.when(owner)
+    def _():
+        total_of(ks.at[pl.ds(0, OWNERS - 1)], 0, n_k1).wait_send()
+        sent("k2", k2.at[pl.ds(1, 15)])
+        sent("k3", k1.at[pl.ds(1, 15)])
+
+    @pl.when(jnp.logical_not(owner))
+    def _():
+        total_of(ks, 0, send_of.pop("k1")).wait_send()
+
+    for out, ref in (("a", a2s), ("b", b2s)):
         sent(out, ref.at[pl.ds(1, 15)])
     sent("ag1", g.at[:, 0, pl.ds(1, 3)])
     sent("ag2", g.at[:, pl.ds(1, 3)])
@@ -397,24 +412,29 @@
     assert not send_of and len(waited) == len(recv_of) + 1
 
 
+def write_out(*refs):
+    copies = [pltpu.make_async_copy(refs[n], refs[n + 4], refs[8].at[n]) for n in range(4)]
+    for copy in copies:
+        copy.start()
+    for copy in copies:
+        copy.wait()
+
+
 def on_device(patches, cotangent, other_logsum, slot_keys, w_in, w_out):
     any_spec = pl.BlockSpec(memory_space=pl.ANY)
     vmem = pl.BlockSpec(memory_space=pltpu.VMEM)
-    patch_grad, key_grad, w_in_grad, w_out_grad = pl.pallas_call(
+    results = pl.pallas_call(
         kernel,
         out_shape=(
-            jax.ShapeDtypeStruct((2, 256, D), BF),
-            jax.ShapeDtypeStruct((32, D), F32),
-            jax.ShapeDtypeStruct((2, FB, D), BF),
-            jax.ShapeDtypeStruct((2, FB, D), BF),
+            pltpu.VMEM((2, 256, D), BF),
+            pltpu.VMEM((32, D), F32),
+            pltpu.VMEM((2, FB, D), BF),
+            pltpu.VMEM((2, FB, D), BF),
         ),
         in_specs=[any_spec, any_spec, vmem, vmem, any_spec, any_spec],
-        out_specs=(any_spec, vmem, any_spec, any_spec),
+        out_specs=(vmem, vmem, vmem, vmem),
         scratch_shapes=[
             pltpu.VMEM((2, 256, D), BF),
-            pltpu.VMEM((2, 256, D), BF),
-            pltpu.VMEM((2, FB, D), BF),
-            pltpu.VMEM((2, FB, D), BF),
             pltpu.VMEM((2, 256, D), BF),
             pltpu.VMEM((2, FB, D), BF),
             pltpu.VMEM((2, FB, D), BF),
@@ -430,21 +450,27 @@
             pltpu.VMEM((16, 16, D // 2), BF),
             pltpu.VMEM((16, 16, D // 2), BF),
             pltpu.VMEM((16, 16, D // 2), BF),
+            pltpu.VMEM((OWNERS, 16, 256), BF),
             pltpu.VMEM((16, 16, 256), BF),
             pltpu.VMEM((16, 16, 256), BF),
-            pltpu.VMEM((16, 16, 256), BF),
-            pltpu.VMEM((16, 16, 256), BF),
-            pltpu.VMEM((16, 16, 256), BF),
+            pltpu.VMEM((OWNERS, 16, 256), BF),
             pltpu.SemaphoreType.DMA((N_SEND,)),
             pltpu.SemaphoreType.DMA((N_RECV,)),
             pltpu.SemaphoreType.DMA((4,)),
-            pltpu.SemaphoreType.DMA((6,)),
         ],
         compiler_params=pltpu.CompilerParams(
-            collective_id=0, has_side_effects=True, vmem_limit_bytes=56 * 2**20
+            collective_id=0, has_side_effects=True, vmem_limit_bytes=58 * 2**20
         ),
         name="soft_moe_backward",
     )(patches, cotangent, other_logsum, slot_keys, jnp.swapaxes(w_in, 1, 2), w_out)
+    patch_grad, key_grad, w_in_grad, w_out_grad = pl.pallas_call(
+        write_out,
+        out_shape=[jax.ShapeDtypeStruct(r.shape, r.dtype) for r in results],
+        in_specs=[vmem] * 4,
+        out_specs=[any_spec] * 4,
+        scratch_shapes=[pltpu.SemaphoreType.DMA((4,))],
+        name="write_out",
+    )(*results)
     return (patch_grad, key_grad, jnp.swapaxes(w_in_grad, 1, 2), w_out_grad)
 
 

time: 128 us -> 129 us (level)
  Pallas kernels: 121 us -> 125 us
  local copies, waits for them, and re-layouts: 6.45 us -> 4.06 us
    pallas_call x1 -> x2, Pallas kernels: 121 us -> 125 us  [the longest x1 120 us: on_device(): pl.pallas_call(kernel, out_shape=(pltpu.VMEM((2, 256, D), BF), pltpu.VMEM...]
    unnamed x10 -> x8, local copies, waits for them, and re-layouts: 6.45 us -> 4.06 us
where the time goes in v3:
time: 129 us
  Pallas kernels  125 us (97%)
  local copies, waits for them, and re-layouts  4.06 us (3%)
    pallas_call x1, Pallas kernels, on_device(): pl.pallas_call(kernel, out_shape=(pltpu.VMEM((2, 256, D), BF), pltpu.VMEM...  120 us
    pallas_call x1, Pallas kernels, on_device(): pl.pallas_call(write_out, out_shape=[jax.ShapeDtypeStruct(r.shape, r.dtyp...  4.64 us
    unnamed x8, local copies, waits for them, and re-layouts  4.06 us

profile of v3, /device:TPU:1, one launch (start us, length us, event | category | flops | bytes accessed | tf_op | source)
XLA Modules:
  0.0 129.3 jit_solution(9320028885919630489)
XLA Ops:
  0.6 119.9 %soft_moe_backward.1 = (bf16[2,256,1280]{2,1,0:T(8,128)(2,1)S(1)}, f32[32,1280]{1,0:T(8,128)S(1)}, bf16[2,320,1280]{2,1,0:T(8,128)(2,1)S(1)}, bf16[2,320,1280]{2,1,0:T(8,128)(2,1)S(1)}) custom-call(bf16[2,256,1280]{2,1,0:T(8,128)(2,1)} %patches_hbm.1, bf16[2,256,1280]{2,1,0:T(8,128)(2,1)} %cot_hbm.1, f32[2,256]{1,0:T(2,128)} %ols_ref.1, ...), custom_call_target="tpu_custom_call" | custom-call | tf_op jit(solution)/shard_map/soft_moe_backward/pallas_call | solution.py:426
  120.6 0.0 copy-start
  120.6 1.2 copy-done
  121.8 0.0 copy-start.1
  121.8 1.2 copy-done.1
  122.9 0.0 copy-start.2
  122.9 1.1 copy-done.2
  124.0 0.0 copy-start.3
  124.0 0.7 copy-done.3
  124.7 4.6 %write_out.1 = (bf16[2,256,1280]{2,1,0:T(8,128)(2,1)}, f32[32,1280]{1,0:T(8,128)}, bf16[2,320,1280]{2,1,0:T(8,128)(2,1)}, bf16[2,320,1280]{2,1,0:T(8,128)(2,1)}) custom-call(bf16[2,256,1280]{2,1,0:T(8,128)(2,1)} %copy-done.2, f32[32,1280]{1,0:T(8,128)} %copy-done.3, bf16[2,320,1280]{2,1,0:T(8,128)(2,1)} %copy-done, bf16[2,320,1280]{2,1,0:T(8,128)(2,1)} %copy-done.1), custom_call_target="tpu_custom_call" | custom-call | tf_op jit(solution)/shard_map/write_out/pallas_call | solution.py:466
Async XLA Ops:
  120.6 1.2 copy-start
  121.8 1.2 copy-start.1
  122.9 1.1 copy-start.2
  124.0 0.7 copy-start.3

commit v4 on v3

--- a/solution.py
+++ b/solution.py
@@ -16,34 +16,36 @@
 SPLIT = 1024
 COLS = {"A": (0, SPLIT), "B": (SPLIT, D - SPLIT)}
 N_RECV = 80
-N_SEND = 10
+N_SEND = 12
+WINDOWS = (0, 384, 768, 896)
 OWNERS = 10
 GELU_C = 0.7978845608028654
 GELU_A = 0.044715
 
 ORDER = (
-    ("ag2", "A", 1, 0), ("ag1", "B", 0), ("ag1", "A", 0), ("ag2", "B", 0, 0), ("ag2", "A", 0, 0), ("ag1", "B", 1),
-    ("ag1", "A", 1), ("ag2_relay", "A", 1, 0), ("ag1_relay", "B", 0), ("ag2", "B", 0, 1), ("ag2_relay", "A", 0, 0),
-    ("ag2", "B", 0, 3), ("ag1_relay", "B", 1), ("ag1_relay", "A", 0), ("ag2", "A", 0, 1), ("ag2", "A", 0, 3),
-    ("ag2_relay", "B", 0, 0), ("ag2", "B", 1, 3), ("ag2", "B", 1, 0), ("ag2_relay", "A", 0, 1),
-    ("ag1_relay", "A", 1), ("ag2", "A", 1, 1), ("ag2", "A", 1, 3), ("ag2_relay", "A", 0, 3),
-    ("ag2_relay", "B", 0, 3), ("ag2_relay", "B", 0, 1), ("ag2", "B", 0, 2), ("ag2", "A", 0, 2), ("ag2", "B", 1, 2),
-    ("expert", 0, 0), ("ag2_relay", "A", 1, 1), ("ag2_relay", "B", 1, 3), ("ag2", "B", 1, 1),
-    ("ag2_relay", "A", 1, 3), ("ag2_relay", "B", 1, 0), ("ag2", "A", 1, 2), ("ag2_relay", "A", 0, 2),
-    ("expert", 0, 1), ("ag2_relay", "B", 0, 2), ("expert", 0, 3), ("rs1_u", "A", 0, 1), ("rs1_u", "A", 0, 2),
-    ("ag2_relay", "B", 1, 1), ("ag2_relay", "B", 1, 2), ("rs1_u", "A", 0, 0), ("rs1_u", "A", 0, 3),
-    ("expert", 1, 0), ("ag2_relay", "A", 1, 2), ("expert", 0, 2), ("rs1_t", "A", 0, 2), ("rs1_t", "B", 0),
-    ("expert", 1, 1), ("rs1_t", "A", 0, 1), ("rs1_u", "B", 0), ("rs1_t", "A", 0, 3), ("expert", 1, 3),
-    ("rs1_u", "A", 1, 2), ("rs1_u", "A", 1, 3), ("expert", 1, 2), ("rs1_u", "B", 1), ("rs1_m", "A", 0, 2),
-    ("rs1_t", "A", 1, 2), ("rs1_t", "B", 1), ("rs1_t", "A", 1, 3), ("rs1_m", "B", 0), ("rs1_t", "A", 1, 1),
-    ("weight_grads", 1), ("rs1_m", "A", 0, 3), ("rs1_m", "A", 0, 1), ("rs1_f", "A", 0, 2), ("rs2_t", "A", 0),
-    ("rs1_u", "A", 1, 0), ("weight_grads", 0), ("rs1_m", "B", 1), ("rs1_f", "B", 0), ("rs2_t", "B", 0),
-    ("rs1_m", "A", 1, 1), ("rs1_f", "A", 0, 3), ("rs1_m", "A", 1, 3), ("rs1_m", "A", 1, 2), ("rs1_f", "A", 0, 1),
-    ("rs2_u", "A", 0), ("rs1_u", "A", 1, 1), ("rs2_u", "B", 0), ("rs2_m", "A", 0), ("rs1_t", "A", 0, 0),
-    ("rs1_t", "A", 1, 0), ("rs2_m", "B", 0), ("rs1_f", "B", 1), ("rs2_t", "B", 1), ("rs2_u", "B", 1),
-    ("rs1_f", "A", 1, 3), ("rs1_f", "A", 1, 2), ("rs2_t", "A", 1), ("rs1_f", "A", 1, 1), ("rs2_u", "A", 1),
-    ("rs1_m", "A", 0, 0), ("rs1_m", "A", 1, 0), ("rs2_f", "B", 0), ("rs2_m", "B", 1), ("rs2_m", "A", 1),
-    ("rs1_f", "A", 0, 0), ("rs2_f", "A", 0), ("rs1_f", "A", 1, 0), ("rs2_f", "B", 1), ("rs2_f", "A", 1),
+    ("a_got", 0), ("ag1", "A", 0), ("ag1", "B", 0), ("ag2", "A", 0, 0), ("a_got", 1), ("ag1_relay", "B", 0),
+    ("ag1", "B", 1), ("ag2", "B", 0, 0), ("ag2", "A", 1, 0), ("ag2", "B", 0, 3), ("ag2_relay", "A", 0, 0),
+    ("ag1_relay", "B", 1), ("ag2", "B", 0, 2), ("ag1_relay", "A", 0), ("ag2", "A", 0, 3), ("ag2", "A", 0, 1),
+    ("ag1", "A", 1), ("ag2_relay", "A", 1, 0), ("ag2_relay", "B", 0, 0), ("ag2", "A", 0, 2), ("ag2", "B", 0, 1),
+    ("ag2_relay", "A", 0, 1), ("ag2_relay", "A", 0, 3), ("ag2", "B", 1, 1), ("ag2_relay", "B", 0, 2),
+    ("ag2_relay", "B", 0, 3), ("ag2", "B", 1, 0), ("ag2_relay", "A", 0, 2), ("ag1_relay", "A", 1),
+    ("ag2", "A", 1, 1), ("expert", 0, 0), ("ag2_relay", "B", 0, 1), ("ag2", "B", 1, 2), ("ag2", "B", 1, 3),
+    ("ag2", "A", 1, 3), ("expert", 0, 2), ("ag2_relay", "B", 1, 0), ("rs1_t", "A", 0, 2), ("ag2_relay", "B", 1, 1),
+    ("ag2_relay", "A", 1, 1), ("expert", 0, 3), ("ag2", "A", 1, 2), ("expert", 0, 1), ("ag2_relay", "B", 1, 2),
+    ("rs1_t", "B", 0), ("rs1_u", "A", 0, 2), ("rs1_m", "A", 0, 2), ("ag2_relay", "A", 1, 3), ("expert", 1, 0),
+    ("ag2_relay", "A", 1, 2), ("rs1_t", "A", 0, 1), ("rs1_u", "B", 0), ("ag2_relay", "B", 1, 3),
+    ("rs1_t", "A", 0, 3), ("expert", 1, 1), ("rs1_f", "A", 0, 2), ("rs1_m", "B", 0), ("rs2_t", "A", 0),
+    ("rs1_u", "A", 0, 3), ("rs1_u", "A", 0, 1), ("expert", 1, 2), ("rs1_t", "A", 1, 2), ("rs1_t", "A", 1, 1),
+    ("expert", 1, 3), ("rs1_t", "B", 1), ("rs1_u", "A", 1, 2), ("rs1_t", "A", 1, 3), ("rs1_m", "A", 1, 2),
+    ("rs1_m", "A", 0, 3), ("rs1_u", "B", 1), ("rs1_m", "A", 0, 1), ("rs1_f", "B", 0), ("rs1_m", "A", 1, 1),
+    ("rs1_u", "A", 1, 3), ("rs1_m", "B", 1), ("rs1_m", "A", 1, 3), ("rs2_u", "B", 0), ("rs2_t", "B", 0),
+    ("rs1_u", "A", 1, 1), ("rs1_t", "A", 0, 0), ("rs1_f", "A", 1, 2), ("rs1_t", "A", 1, 0), ("rs2_t", "A", 1),
+    ("rs1_f", "A", 0, 3), ("rs1_u", "A", 0, 0), ("rs1_f", "A", 0, 1), ("rs2_m", "A", 0), ("rs2_u", "A", 0),
+    ("weight_grads", 0), ("rs1_f", "B", 1), ("rs1_f", "A", 1, 3), ("rs2_t", "B", 1), ("rs1_f", "A", 1, 1),
+    ("rs2_u", "A", 1), ("rs2_m", "A", 1), ("rs2_m", "B", 0), ("rs1_m", "A", 0, 0), ("rs1_m", "A", 1, 0),
+    ("rs1_u", "A", 1, 0), ("rs2_m", "B", 1), ("rs2_f", "B", 0), ("rs2_u", "B", 1), ("rs1_f", "A", 0, 0),
+    ("rs2_f", "A", 0), ("b_send", 0), ("rs1_f", "A", 1, 0), ("rs2_f", "B", 1), ("rs2_f", "A", 1), ("b_send", 1),
+    ("weight_grads", 1),
 )
 
 
@@ -63,26 +65,15 @@
     return lax.broadcasted_iota(jnp.int32, shape, dim)
 
 
-def piece_row(slot_off, half, k, t, i):
-    return slot_off * 16 + half * 8 + k * 4 + t * 2 + i
-
-
-def spread_index(r, me):
-    off, k, t, i = r >> 4, (r >> 2) & 1, (r >> 1) & 1, r & 1
-    owner = (me + off) & 15
-    return (t * 2 + i) * 32 + 2 * owner + k
-
-
-def block_index(r):
-    off, k, t, i = r >> 4, (r >> 2) & 1, (r >> 1) & 1, r & 1
-    return (k * 2 + t) * 32 + off * 2 + i
-
-
-def one_hot(index_of, half, rows_are_pieces):
-    shape = (256, 128) if rows_are_pieces else (128, 256)
-    piece = iota(shape, 0 if rows_are_pieces else 1)
-    other = iota(shape, 1 if rows_are_pieces else 0)
-    hit = (index_of(piece) == other) & (((piece >> 3) & 1) == half)
+def piece_parts(r):
+    return r >> 4, (r >> 2) & 3, (r >> 1) & 1, r & 1
+
+
+def one_hot(index_of, window, others, pieces_first):
+    shape = (256, others) if pieces_first else (others, 256)
+    piece = iota(shape, 0 if pieces_first else 1)
+    other = iota(shape, 1 if pieces_first else 0)
+    hit = (index_of(piece) == other) & (piece_parts(piece)[1] == window)
     return jnp.where(hit, 1.0, 0.0).astype(BF)
 
 
@@ -163,27 +154,46 @@
         rows_grad.append(dot(combine.astype(BF), cot[i]).astype(BF))
     rows = jnp.concatenate(rows_in + rows_grad, axis=0)
 
+    def spread(k):
+        def index(r):
+            off, _, t, i = piece_parts(r)
+            return (t * 2 + i) * 32 + 2 * ((me + off) & 15) + k
+
+        return index
+
+    def in_block(r):
+        off, _, t, i = piece_parts(r)
+        return t * 32 + off * 2 + i
+
     def to_pieces(rows, index_of, dst):
-        half = D // 2
-        pieces = dot(one_hot(index_of, 0, True), rows[:, :half]) + dot(
-            one_hot(index_of, 1, True), rows[:, half:]
-        )
-        dst[...] = pieces.astype(BF).reshape(16, 16, half)
-
-    def from_pieces(src, index_of, half):
-        pieces = src[...].reshape(256, D // 2)
-        return dot(one_hot(index_of, half, False), pieces).astype(BF)
-
-    spread = functools.partial(spread_index, me=me)
-    to_pieces(rows, spread, a2s)
-    a2r[0] = a2s[0]
+        total = jnp.zeros((256, 384), F32)
+        for w, c0 in enumerate(WINDOWS):
+            total = total + dot(one_hot(index_of, w, rows.shape[0], True), rows[:, c0 : c0 + 384])
+        dst[...] = total.astype(BF).reshape(16, 16, 384)
+
+    def from_pieces(src, index_of, window, others):
+        return dot(one_hot(index_of, window, others, False), src[...].reshape(256, 384))
+
     pl.semaphore_wait(barrier, 30)
-    for off in range(1, 16):
-        send("a", "a", a2s.at[off], a2r.at[off], expert_peer(off))
-    got("a", a2r.at[pl.ds(1, 15)])
-    for half in range(2):
-        cols = slice(half * 640, half * 640 + 640)
-        g[:, 0, 0, :, cols] = from_pieces(a2r, block_index, half).reshape(4, 32, 640)
+    for k in range(2):
+        to_pieces(rows, spread(k), a2s.at[k])
+        a2r[k, 0] = a2s[k, 0]
+        for off in range(1, 16):
+            send(("a", k), ("a", k), a2s.at[k, off], a2r.at[k, off], expert_peer(off))
+
+    def a_got(k):
+        got(("a", k), a2r.at[k, pl.ds(1, 15)])
+        for w, c0 in enumerate(WINDOWS):
+            block = from_pieces(a2r.at[k], in_block, w, 64).astype(BF)
+            if w == 3:
+                block, c0 = block[:, 256:], c0 + 256
+            g[2 * k : 2 * k + 2, 0, 0, :, c0 : c0 + block.shape[1]] = block.reshape(2, 32, block.shape[1])
+
+    def b_send(k):
+        to_pieces(pt[2 * k : 2 * k + 2, 0, 0].reshape(64, D), in_block, b2s.at[k])
+        b2r[k, 0] = b2s[k, 0]
+        for off in range(1, 16):
+            send(("b", k), ("b", k), b2s.at[k, off], b2r.at[k, off], expert_peer(16 - off))
 
     AXES = {"A": ("z", "y"), "B": ("y", "z")}
 
@@ -306,19 +316,20 @@
         for u, m, r0 in ((UP, MM, 0), (UM, MP, 16)):
             add_into(part_of(ph, part, k, a1, 0, r0), land(ph, part, k, a1, u), land(ph, part, k, a1, m))
 
-    steps = {"ag1": ag1, "ag1_relay": ag1_relay, "ag2": ag2, "ag2_relay": ag2_relay, "expert": expert, "weight_grads": weight_grads}
+    steps = {"ag1": ag1, "ag1_relay": ag1_relay, "ag2": ag2, "ag2_relay": ag2_relay, "expert": expert, "weight_grads": weight_grads, "a_got": a_got, "b_send": b_send}
     for ph in (1, 2):
         for name, step in (("t", rs_t), ("u", rs_u), ("m", rs_m), ("f", rs_f)):
             steps["rs%d_%s" % (ph, name)] = functools.partial(step, ph)
     for name, *where in ORDER:
         steps[name](*where)
 
-    to_pieces(pt[:, 0, 0].reshape(128, D), block_index, b2s)
-    b2r[0] = b2s[0]
-    for off in range(1, 16):
-        send("b", "b", b2s.at[off], b2r.at[off], expert_peer(16 - off))
-    got("b", b2r.at[pl.ds(1, 15)])
-    back = jnp.concatenate([from_pieces(b2r, spread, half) for half in range(2)], axis=1)
+    for k in range(2):
+        got(("b", k), b2r.at[k, pl.ds(1, 15)])
+    back = []
+    for w in range(4):
+        cols = sum(from_pieces(b2r.at[k], spread(k), w, 128) for k in range(2)).astype(BF)
+        back.append(cols[:, 256:] if w == 3 else cols)
+    back = jnp.concatenate(back, axis=1)
 
     halves = []
     key_part = jnp.zeros((32, D), F32)
@@ -403,8 +414,9 @@
     def _():
         total_of(ks, 0, send_of.pop("k1")).wait_send()
 
-    for out, ref in (("a", a2s), ("b", b2s)):
-        sent(out, ref.at[pl.ds(1, 15)])
+    for k in range(2):
+        sent(("a", k), a2s.at[k, pl.ds(1, 15)])
+        sent(("b", k), b2s.at[k, pl.ds(1, 15)])
     sent("ag1", g.at[:, 0, pl.ds(1, 3)])
     sent("ag2", g.at[:, pl.ds(1, 3)])
     sent(("rs", 1), r1)
@@ -446,10 +458,10 @@
             pltpu.VMEM((2, 512, FB), BF),
             pltpu.VMEM((2, 6, 2, 4, 16, D), BF),
             pltpu.VMEM((2, 6, 2, 16, D), BF),
-            pltpu.VMEM((16, 16, D // 2), BF),
-            pltpu.VMEM((16, 16, D // 2), BF),
-            pltpu.VMEM((16, 16, D // 2), BF),
-            pltpu.VMEM((16, 16, D // 2), BF),
+            pltpu.VMEM((2, 16, 16, 384), BF),
+            pltpu.VMEM((2, 16, 16, 384), BF),
+            pltpu.VMEM((2, 16, 16, 384), BF),
+            pltpu.VMEM((2, 16, 16, 384), BF),
             pltpu.VMEM((OWNERS, 16, 256), BF),
             pltpu.VMEM((16, 16, 256), BF),
             pltpu.VMEM((16, 16, 256), BF),
@@ -466,9 +478,10 @@
     patch_grad, key_grad, w_in_grad, w_out_grad = pl.pallas_call(
         write_out,
         out_shape=[jax.ShapeDtypeStruct(r.shape, r.dtype) for r in results],
-        in_specs=[vmem] * 4,
+        in_specs=[any_spec] * 4,
         out_specs=[any_spec] * 4,
         scratch_shapes=[pltpu.SemaphoreType.DMA((4,))],
+        compiler_params=pltpu.CompilerParams(vmem_limit_bytes=8 * 2**20),
         name="write_out",
     )(*results)
     return (patch_grad, key_grad, jnp.swapaxes(w_in_grad, 1, 2), w_out_grad)

time: 129 us -> 120 us (0.930)
  Pallas kernels: 125 us -> 119 us
  local copies, waits for them, and re-layouts: 4.06 us -> 0 us
    unnamed x8 -> x0, local copies, waits for them, and re-layouts: 4.06 us -> none
    pallas_call x1, Pallas kernels: 120 us -> 117 us  [on_device(): pl.pallas_call(kernel, out_shape=(pltpu.VMEM((2, 256, D), BF), pltpu.VMEM...]
    pallas_call x1, Pallas kernels: 4.64 us -> 2.23 us  [on_device(): pl.pallas_call(write_out, out_shape=[jax.ShapeDtypeStruct(r.shape, r.dtyp...]
where the time goes in v4:
time: 120 us
  Pallas kernels  119 us (99%)
    pallas_call x1, Pallas kernels, on_device(): pl.pallas_call(kernel, out_shape=(pltpu.VMEM((2, 256, D), BF), pltpu.VMEM...  117 us

profile of v4, /device:TPU:1, one launch (start us, length us, event | category | flops | bytes accessed | tf_op | source)
XLA Modules:
  0.0 120.0 jit_solution(11473149920763790298)
XLA Ops:
  0.6 117.1 %soft_moe_backward.1 = (bf16[2,256,1280]{2,1,0:T(8,128)(2,1)S(1)}, f32[32,1280]{1,0:T(8,128)S(1)}, bf16[2,320,1280]{2,1,0:T(8,128)(2,1)S(1)}, bf16[2,320,1280]{2,1,0:T(8,128)(2,1)S(1)}) custom-call(bf16[2,256,1280]{2,1,0:T(8,128)(2,1)} %patches_hbm.1, bf16[2,256,1280]{2,1,0:T(8,128)(2,1)} %cot_hbm.1, f32[2,256]{1,0:T(2,128)} %ols_ref.1, ...), custom_call_target="tpu_custom_call" | custom-call | tf_op jit(solution)/shard_map/soft_moe_backward/pallas_call | solution.py:438
  117.8 2.2 %write_out.1 = (bf16[2,256,1280]{2,1,0:T(8,128)(2,1)}, f32[32,1280]{1,0:T(8,128)}, bf16[2,320,1280]{2,1,0:T(8,128)(2,1)}, bf16[2,320,1280]{2,1,0:T(8,128)(2,1)}) custom-call(bf16[2,256,1280]{2,1,0:T(8,128)(2,1)S(1)} %get-tuple-element.12.refs_0_, f32[32,1280]{1,0:T(8,128)S(1)} %get-tuple-element.13.refs_1_, ...), custom_call_target="tpu_custom_call" | custom-call | tf_op jit(solution)/shard_map/write_out/pallas_call | solution.py:478

commit v5 on v4

--- a/solution.py
+++ b/solution.py
@@ -23,28 +23,28 @@
 GELU_A = 0.044715
 
 ORDER = (
-    ("a_got", 0), ("ag1", "A", 0), ("ag1", "B", 0), ("ag2", "A", 0, 0), ("a_got", 1), ("ag1_relay", "B", 0),
-    ("ag1", "B", 1), ("ag2", "B", 0, 0), ("ag2", "A", 1, 0), ("ag2", "B", 0, 3), ("ag2_relay", "A", 0, 0),
-    ("ag1_relay", "B", 1), ("ag2", "B", 0, 2), ("ag1_relay", "A", 0), ("ag2", "A", 0, 3), ("ag2", "A", 0, 1),
-    ("ag1", "A", 1), ("ag2_relay", "A", 1, 0), ("ag2_relay", "B", 0, 0), ("ag2", "A", 0, 2), ("ag2", "B", 0, 1),
-    ("ag2_relay", "A", 0, 1), ("ag2_relay", "A", 0, 3), ("ag2", "B", 1, 1), ("ag2_relay", "B", 0, 2),
-    ("ag2_relay", "B", 0, 3), ("ag2", "B", 1, 0), ("ag2_relay", "A", 0, 2), ("ag1_relay", "A", 1),
-    ("ag2", "A", 1, 1), ("expert", 0, 0), ("ag2_relay", "B", 0, 1), ("ag2", "B", 1, 2), ("ag2", "B", 1, 3),
-    ("ag2", "A", 1, 3), ("expert", 0, 2), ("ag2_relay", "B", 1, 0), ("rs1_t", "A", 0, 2), ("ag2_relay", "B", 1, 1),
-    ("ag2_relay", "A", 1, 1), ("expert", 0, 3), ("ag2", "A", 1, 2), ("expert", 0, 1), ("ag2_relay", "B", 1, 2),
-    ("rs1_t", "B", 0), ("rs1_u", "A", 0, 2), ("rs1_m", "A", 0, 2), ("ag2_relay", "A", 1, 3), ("expert", 1, 0),
-    ("ag2_relay", "A", 1, 2), ("rs1_t", "A", 0, 1), ("rs1_u", "B", 0), ("ag2_relay", "B", 1, 3),
-    ("rs1_t", "A", 0, 3), ("expert", 1, 1), ("rs1_f", "A", 0, 2), ("rs1_m", "B", 0), ("rs2_t", "A", 0),
-    ("rs1_u", "A", 0, 3), ("rs1_u", "A", 0, 1), ("expert", 1, 2), ("rs1_t", "A", 1, 2), ("rs1_t", "A", 1, 1),
-    ("expert", 1, 3), ("rs1_t", "B", 1), ("rs1_u", "A", 1, 2), ("rs1_t", "A", 1, 3), ("rs1_m", "A", 1, 2),
-    ("rs1_m", "A", 0, 3), ("rs1_u", "B", 1), ("rs1_m", "A", 0, 1), ("rs1_f", "B", 0), ("rs1_m", "A", 1, 1),
-    ("rs1_u", "A", 1, 3), ("rs1_m", "B", 1), ("rs1_m", "A", 1, 3), ("rs2_u", "B", 0), ("rs2_t", "B", 0),
-    ("rs1_u", "A", 1, 1), ("rs1_t", "A", 0, 0), ("rs1_f", "A", 1, 2), ("rs1_t", "A", 1, 0), ("rs2_t", "A", 1),
-    ("rs1_f", "A", 0, 3), ("rs1_u", "A", 0, 0), ("rs1_f", "A", 0, 1), ("rs2_m", "A", 0), ("rs2_u", "A", 0),
-    ("weight_grads", 0), ("rs1_f", "B", 1), ("rs1_f", "A", 1, 3), ("rs2_t", "B", 1), ("rs1_f", "A", 1, 1),
-    ("rs2_u", "A", 1), ("rs2_m", "A", 1), ("rs2_m", "B", 0), ("rs1_m", "A", 0, 0), ("rs1_m", "A", 1, 0),
-    ("rs1_u", "A", 1, 0), ("rs2_m", "B", 1), ("rs2_f", "B", 0), ("rs2_u", "B", 1), ("rs1_f", "A", 0, 0),
-    ("rs2_f", "A", 0), ("b_send", 0), ("rs1_f", "A", 1, 0), ("rs2_f", "B", 1), ("rs2_f", "A", 1), ("b_send", 1),
+    ("a_got", 0), ("ag2", "A", 0, 0), ("ag1", "A", 0), ("a_got", 1), ("ag2", "A", 1, 0), ("ag1", "A", 1),
+    ("ag1", "B", 1), ("ag1", "B", 0), ("ag2_relay", "A", 0, 0), ("ag2_relay", "A", 1, 0), ("ag1_relay", "B", 1),
+    ("ag1_relay", "A", 0), ("ag1_relay", "B", 0), ("ag2", "A", 0, 1), ("ag2", "A", 0, 3), ("ag2", "B", 0, 3),
+    ("ag1_relay", "A", 1), ("ag2", "A", 1, 1), ("ag2", "A", 0, 2), ("ag2", "B", 1, 3), ("ag2", "B", 0, 2),
+    ("ag2", "B", 0, 1), ("ag2_relay", "A", 0, 1), ("ag2", "B", 1, 1), ("ag2", "B", 0, 0), ("ag2", "A", 1, 3),
+    ("ag2_relay", "B", 1, 3), ("ag2", "A", 1, 2), ("ag2_relay", "B", 0, 1), ("ag2_relay", "B", 0, 3),
+    ("ag2_relay", "A", 1, 1), ("ag2_relay", "A", 0, 3), ("ag2", "B", 1, 0), ("ag2_relay", "A", 0, 2),
+    ("ag2", "B", 1, 2), ("ag2_relay", "B", 0, 0), ("ag2_relay", "B", 0, 2), ("ag2_relay", "B", 1, 1),
+    ("expert", 0, 3), ("ag2_relay", "A", 1, 3), ("expert", 0, 1), ("ag2_relay", "B", 1, 0), ("rs1_u", "A", 0, 3),
+    ("ag2_relay", "A", 1, 2), ("rs1_u", "A", 0, 2), ("ag2_relay", "B", 1, 2), ("expert", 0, 0), ("expert", 0, 2),
+    ("rs1_t", "B", 0), ("rs1_t", "A", 0, 1), ("rs1_u", "B", 0), ("expert", 1, 1), ("rs1_t", "A", 0, 3),
+    ("expert", 1, 0), ("rs1_t", "A", 0, 2), ("expert", 1, 2), ("expert", 1, 3), ("rs1_t", "A", 1, 2),
+    ("rs1_t", "B", 1), ("rs1_t", "A", 1, 1), ("rs1_m", "B", 0), ("weight_grads", 0), ("rs1_u", "A", 0, 1),
+    ("rs1_u", "A", 1, 2), ("rs1_m", "A", 0, 2), ("rs1_u", "B", 1), ("rs1_t", "A", 1, 3), ("rs1_m", "B", 1),
+    ("rs1_m", "A", 1, 2), ("rs1_m", "A", 0, 1), ("rs1_m", "A", 0, 3), ("rs1_m", "A", 1, 1), ("rs1_f", "B", 0),
+    ("rs1_u", "A", 1, 1), ("rs1_f", "A", 0, 2), ("rs2_t", "A", 0), ("rs1_f", "A", 1, 2), ("rs2_t", "A", 1),
+    ("rs2_t", "B", 0), ("rs1_m", "A", 1, 3), ("rs1_f", "A", 0, 3), ("rs1_f", "B", 1), ("rs1_f", "A", 0, 1),
+    ("rs2_u", "A", 0), ("rs1_u", "A", 1, 3), ("rs2_u", "B", 0), ("rs1_t", "A", 0, 0), ("rs1_t", "A", 1, 0),
+    ("rs1_u", "A", 0, 0), ("rs2_m", "A", 0), ("rs2_t", "B", 1), ("rs1_f", "A", 1, 1), ("rs1_f", "A", 1, 3),
+    ("rs2_u", "A", 1), ("rs2_m", "B", 0), ("rs1_m", "A", 0, 0), ("rs2_m", "A", 1), ("rs1_m", "A", 1, 0),
+    ("rs1_u", "A", 1, 0), ("rs2_m", "B", 1), ("rs2_u", "B", 1), ("rs2_f", "B", 0), ("rs1_f", "A", 0, 0),
+    ("rs2_f", "A", 0), ("b_send", 0), ("rs1_f", "A", 1, 0), ("rs2_f", "A", 1), ("rs2_f", "B", 1), ("b_send", 1),
     ("weight_grads", 1),
 )
 
@@ -83,6 +83,7 @@
     patches, cot, win, wout,
     disp_s, comb_s, g, pt, act_s, pre_s, r1, r2,
     a2s, a2r, b2s, b2r, ks, k1, k2, k3,
+    hot_out, hot_in, hot_ret, hot_back,
     send_sem, recv_sem, in_sem,
 ):
     dp = lax.axis_index("dp")
@@ -106,12 +107,14 @@
         pl.semaphore_signal(barrier, inc=1, device_id=dp_peer(off), device_id_type=MESH)
 
     loads = {}
-    for n, (name, src, dst) in enumerate(
-        (("x", patches_hbm, patches), ("c", cot_hbm, cot), ("wi", win_hbm, win), ("wo", wout_hbm, wout))
-    ):
+    for n, (name, src, dst) in enumerate((
+        ("x0", patches_hbm.at[0], patches.at[0]), ("x1", patches_hbm.at[1], patches.at[1]),
+        ("c0", cot_hbm.at[0], cot.at[0]), ("c1", cot_hbm.at[1], cot.at[1]),
+        ("wi", win_hbm, win), ("wo", wout_hbm, wout),
+    )):
         loads[name] = pltpu.make_async_copy(src, dst, in_sem.at[n])
-    loads["x"].start()
-    loads["c"].start()
+        if n < 4:
+            loads[name].start()
 
     recv_of, send_of, waited = {}, {}, set()
 
@@ -138,59 +141,70 @@
     def sent(out, ref):
         total_of(ref, 0, send_of.pop(out)).wait_send()
 
+    def spread(k):
+        def index(r):
+            off, _, t, i = piece_parts(r)
+            return (t * 2 + i) * 32 + 2 * ((me + off) & 15) + k
+
+        return index
+
+    def in_block(r):
+        off, _, t, i = piece_parts(r)
+        return t * 32 + off * 2 + i
+
+    def spread_hots(k):
+        for w in range(4):
+            hot_out[4 * k + w] = one_hot(spread(k), w, 128, True)
+
+    spread_hots(0)
     keys = keys_ref[...]
-    loads["x"].wait()
-    loads["c"].wait()
-    loads["wi"].start()
-    loads["wo"].start()
-    rows_in, rows_grad = [], []
+    rows_in, rows_grad, combines = [], [], []
     for i in range(2):
+        loads["x%d" % i].wait()
         exponent = jnp.exp(dot_nt(keys, patches[i]))
         dispatch = exponent / jnp.sum(exponent, axis=1, keepdims=True)
         combine = exponent / (jnp.sum(exponent, axis=0, keepdims=True) + jnp.exp(ols_ref[i : i + 1, :]))
         disp_s[i] = dispatch
         comb_s[i] = combine
         rows_in.append(dot(dispatch.astype(BF), patches[i]).astype(BF))
-        rows_grad.append(dot(combine.astype(BF), cot[i]).astype(BF))
+        combines.append(combine.astype(BF))
+    for i in range(2):
+        loads["c%d" % i].wait()
+        rows_grad.append(dot(combines[i], cot[i]).astype(BF))
+    loads["wi"].start()
+    loads["wo"].start()
     rows = jnp.concatenate(rows_in + rows_grad, axis=0)
 
-    def spread(k):
-        def index(r):
-            off, _, t, i = piece_parts(r)
-            return (t * 2 + i) * 32 + 2 * ((me + off) & 15) + k
-
-        return index
-
-    def in_block(r):
-        off, _, t, i = piece_parts(r)
-        return t * 32 + off * 2 + i
-
-    def to_pieces(rows, index_of, dst):
+    def to_pieces(rows, hots, dst):
         total = jnp.zeros((256, 384), F32)
         for w, c0 in enumerate(WINDOWS):
-            total = total + dot(one_hot(index_of, w, rows.shape[0], True), rows[:, c0 : c0 + 384])
+            total = total + dot(hots[w], rows[:, c0 : c0 + 384])
         dst[...] = total.astype(BF).reshape(16, 16, 384)
-
-    def from_pieces(src, index_of, window, others):
-        return dot(one_hot(index_of, window, others, False), src[...].reshape(256, 384))
 
     pl.semaphore_wait(barrier, 30)
     for k in range(2):
-        to_pieces(rows, spread(k), a2s.at[k])
+        if k == 1:
+            spread_hots(1)
+        to_pieces(rows, hot_out.at[pl.ds(4 * k, 4)], a2s.at[k])
         a2r[k, 0] = a2s[k, 0]
         for off in range(1, 16):
             send(("a", k), ("a", k), a2s.at[k, off], a2r.at[k, off], expert_peer(off))
+    for w in range(4):
+        hot_in[w] = one_hot(in_block, w, 64, False)
+        hot_ret[w] = one_hot(in_block, w, 64, True)
+        for k in range(2):
+            hot_back[4 * k + w] = one_hot(spread(k), w, 128, False)
 
     def a_got(k):
         got(("a", k), a2r.at[k, pl.ds(1, 15)])
         for w, c0 in enumerate(WINDOWS):
-            block = from_pieces(a2r.at[k], in_block, w, 64).astype(BF)
+            block = dot(hot_in[w], a2r[k].reshape(256, 384)).astype(BF)
             if w == 3:
                 block, c0 = block[:, 256:], c0 + 256
             g[2 * k : 2 * k + 2, 0, 0, :, c0 : c0 + block.shape[1]] = block.reshape(2, 32, block.shape[1])
 
     def b_send(k):
-        to_pieces(pt[2 * k : 2 * k + 2, 0, 0].reshape(64, D), in_block, b2s.at[k])
+        to_pieces(pt[2 * k : 2 * k + 2, 0, 0].reshape(64, D), hot_ret, b2s.at[k])
         b2r[k, 0] = b2s[k, 0]
         for off in range(1, 16):
             send(("b", k), ("b", k), b2s.at[k, off], b2r.at[k, off], expert_peer(16 - off))
@@ -323,13 +337,13 @@
     for name, *where in ORDER:
         steps[name](*where)
 
+    back = [jnp.zeros((128, 384), F32)] * 4
     for k in range(2):
         got(("b", k), b2r.at[k, pl.ds(1, 15)])
-    back = []
-    for w in range(4):
-        cols = sum(from_pieces(b2r.at[k], spread(k), w, 128) for k in range(2)).astype(BF)
-        back.append(cols[:, 256:] if w == 3 else cols)
-    back = jnp.concatenate(back, axis=1)
+        pieces = b2r[k].reshape(256, 384)
+        back = [back[w] + dot(hot_back[4 * k + w], pieces) for w in range(4)]
+    back[3] = back[3][:, 256:]
+    back = jnp.concatenate([b.astype(BF) for b in back], axis=1)
 
     halves = []
     key_part = jnp.zeros((32, D), F32)
@@ -466,9 +480,13 @@
             pltpu.VMEM((16, 16, 256), BF),
             pltpu.VMEM((16, 16, 256), BF),
             pltpu.VMEM((OWNERS, 16, 256), BF),
+            pltpu.VMEM((8, 256, 128), BF),
+            pltpu.VMEM((4, 64, 256), BF),
+            pltpu.VMEM((4, 256, 64), BF),
+            pltpu.VMEM((8, 128, 256), BF),
             pltpu.SemaphoreType.DMA((N_SEND,)),
             pltpu.SemaphoreType.DMA((N_RECV,)),
-            pltpu.SemaphoreType.DMA((4,)),
+            pltpu.SemaphoreType.DMA((6,)),
         ],
         compiler_params=pltpu.CompilerParams(
             collective_id=0, has_side_effects=True, vmem_limit_bytes=58 * 2**20

time: 120 us -> 119 us (level)
    pallas_call x1, Pallas kernels: 117 us -> 116 us  [on_device(): pl.pallas_call(kernel, out_shape=(pltpu.VMEM((2, 256, D), BF), pltpu.VMEM...]
where the time goes in v5:
time: 119 us
  Pallas kernels  118 us (99%)
    pallas_call x1, Pallas kernels, on_device(): pl.pallas_call(kernel, out_shape=(pltpu.VMEM((2, 256, D), BF), pltpu.VMEM...  116 us

profile of v5, /device:TPU:1, one launch (start us, length us, event | category | flops | bytes accessed | tf_op | source)
XLA Modules:
  0.0 118.8 jit_solution(7496661547045754267)
XLA Ops:
  0.6 115.8 %soft_moe_backward.1 = (bf16[2,256,1280]{2,1,0:T(8,128)(2,1)S(1)}, f32[32,1280]{1,0:T(8,128)S(1)}, bf16[2,320,1280]{2,1,0:T(8,128)(2,1)S(1)}, bf16[2,320,1280]{2,1,0:T(8,128)(2,1)S(1)}) custom-call(bf16[2,256,1280]{2,1,0:T(8,128)(2,1)} %patches_hbm.1, bf16[2,256,1280]{2,1,0:T(8,128)(2,1)} %cot_hbm.1, f32[2,256]{1,0:T(2,128)} %ols_ref.1, ...), custom_call_target="tpu_custom_call" | custom-call | tf_op jit(solution)/shard_map/soft_moe_backward/pallas_call | solution.py:452
  116.4 2.2 %write_out.1 = (bf16[2,256,1280]{2,1,0:T(8,128)(2,1)}, f32[32,1280]{1,0:T(8,128)}, bf16[2,320,1280]{2,1,0:T(8,128)(2,1)}, bf16[2,320,1280]{2,1,0:T(8,128)(2,1)}) custom-call(bf16[2,256,1280]{2,1,0:T(8,128)(2,1)S(1)} %get-tuple-element.12.refs_0_, f32[32,1280]{1,0:T(8,128)S(1)} %get-tuple-element.13.refs_1_, ...), custom_call_target="tpu_custom_call" | custom-call | tf_op jit(solution)/shard_map/write_out/pallas_call | solution.py:496
